TPU v7x, 32 devices: a whole 2x2x4 slice. The times are simulated.
32 devices in a mesh: groups: 2 (over y), seq: 4 (over z), head: 2 (over x), rep: 2 (over core).
Axes of the slice: x: 2, y: 2, z: 4, core: 2. Of those that a mesh axis runs over, the one named last changes fastest.
Arguments:
- queries: bfloat16 [32768, 16, 128], P(('groups', 'seq'), ('head', 'rep')), parts along dimension 0, may hold values from -8 to 8
- keys: bfloat16 [32768, 128], P(('groups', 'seq')), parts along dimension 0, may hold values from -6 to 6
- values: bfloat16 [32768, 128], P(('groups', 'seq')), parts along dimension 0, may hold values from -6 to 6
- query_maps: bfloat16 [32, 128, 128], P(('groups', 'head', 'rep')), parts along dimension 0, may hold values from -0.5 to 0.5
- key_map: bfloat16 [256, 128], P('groups'), parts along dimension 0, may hold values from -0.046875 to 0.046875
- linear_cotangent: bfloat16 [32768, 16, 128], P(('groups', 'seq'), ('head', 'rep')), parts along dimension 0, may hold values from -0.046875 to 0.046875
Outputs:
- softmax_out: bfloat16 [32768, 16, 128], P(('groups', 'seq'), ('head', 'rep')), parts along dimension 0
- linear_out: bfloat16 [32768, 16, 128], P(('groups', 'seq'), ('head', 'rep')), parts along dimension 0
- map_gradient: float32 [256, 16, 128], P(('groups', 'seq'), ('head', 'rep')), parts along dimension 0
There are 2 independent parts, one for each index of `groups`. A program takes and returns all parts, laid end to end along the dimension named above; each array names one. Nothing has to cross between parts.
All inputs are finite; a program needn't handle non-finite values.
Results may differ from a plain program's by a relative error of at most 0.0058.
Values may be sent and summed in bfloat16 or wider, within the bound.
No kernel may reach another device: no remote copies, remote signals or barrier semaphores. Data moves between devices by JAX's collectives and lax.ppermute only.
A program may use at most 128 MiB of HBM per device.

v0:
```python
import jax
import jax.numpy as jnp
from jax import lax
from jax.sharding import PartitionSpec as P

W = 512


def from_behind(value, axis, steps):
    count = lax.axis_size(axis)
    leading, last = (max(0, -steps), min(count, count - steps))
    return lax.ppermute(value, axis, [(source, source + steps) for source in range(leading, last)])


def carried_in(array, axis, combine, identity):
    count, mine = (lax.axis_size(axis), lax.axis_index(axis))
    everything = lax.all_gather(array, axis)
    start = jnp.broadcast_to(jnp.asarray(identity, array.dtype), array.shape)

    def lap(k, before):
        reached = k < mine
        new = combine(before, everything[k])
        return jnp.where(reached, new, before)

    return lax.fori_loop(0, count, lap, start)


def window_block(block_index, start_state, tensors, position_base):
    queries, keys_ext, values_ext, query_features, key_features, values, cotangent = tensors
    highest_precision = lax.Precision.HIGHEST
    first_row = block_index * W
    head_dim = keys_ext.shape[1]
    query_block = lax.dynamic_slice_in_dim(queries, first_row, W, 0)
    key_window = lax.dynamic_slice_in_dim(keys_ext, first_row, 2 * W, 0)
    value_window = lax.dynamic_slice_in_dim(values_ext, first_row, 2 * W, 0)
    query_pos = position_base + first_row + jnp.arange(W, dtype=jnp.int32)
    key_pos = position_base + first_row - W + jnp.arange(2 * W, dtype=jnp.int32)
    spacing = query_pos[:, None] - key_pos[None, :]
    allowed = (spacing >= 0) & (spacing < W) & (key_pos[None, :] >= 0)
    scores = jnp.einsum(
        "whd,kd->hwk", query_block, key_window, preferred_element_type=jnp.float32
    ) * head_dim ** (-0.5)
    scores = jnp.where(allowed[None], scores, -1e30)
    highest = jnp.max(scores, axis=2, keepdims=True)
    shifted_exp = jnp.exp(scores - highest)
    weights = (shifted_exp / jnp.sum(shifted_exp, axis=2, keepdims=True)).astype(jnp.bfloat16)
    soft_block = jnp.einsum(
        "hwk,kd->whd", weights, value_window, preferred_element_type=jnp.float32
    ).astype(jnp.bfloat16)
    feature_block = lax.dynamic_slice_in_dim(query_features, first_row, W, 0)
    key_block = lax.dynamic_slice_in_dim(key_features, first_row, W, 0)
    value_block = lax.dynamic_slice_in_dim(values, first_row, W, 0)
    cotangent_block = lax.dynamic_slice_in_dim(cotangent, first_row, W, 0)
    causal = jnp.arange(W)[:, None] >= jnp.arange(W)[None, :]
    factor = lax.rsqrt((query_pos + 1).astype(jnp.float32))[:, None, None]
    linear_scores = jnp.where(
        causal[None],
        jnp.einsum("whf,sf->hws", feature_block, key_block, preferred_element_type=jnp.float32),
        0.0,
    ).astype(jnp.bfloat16)
    inside = jnp.einsum(
        "hws,sd->whd", linear_scores, value_block, preferred_element_type=jnp.float32
    )
    carried = jnp.einsum(
        "whf,fd->whd", feature_block.astype(jnp.float32), start_state, precision=highest_precision
    )
    linear_block = (factor * (inside + carried)).astype(jnp.bfloat16)
    back_scores = jnp.where(
        causal[None],
        jnp.einsum("whd,sd->hws", cotangent_block, value_block, preferred_element_type=jnp.float32),
        0.0,
    ).astype(jnp.bfloat16)
    back_inside = jnp.einsum(
        "hws,sf->whf", back_scores, key_block, preferred_element_type=jnp.float32
    )
    back_carried = jnp.einsum(
        "whd,fd->whf", cotangent_block.astype(jnp.float32), start_state, precision=highest_precision
    )
    feature_gradient = (factor * (back_inside + back_carried)).astype(jnp.bfloat16)
    return (soft_block, linear_block, feature_gradient)


def per_device(queries, keys, values, query_maps, key_map, linear_cotangent):
    tokens_here = keys.shape[0]
    head_dim = keys.shape[1]
    heads_here = queries.shape[1]
    block_count = tokens_here // W
    seq_rank = lax.axis_index("seq")
    rim_keys, rim_values = from_behind(
        (keys[tokens_here - W :], values[tokens_here - W :]), "seq", 1
    )
    keys_ext = jnp.concatenate([rim_keys, keys], axis=0)
    values_ext = jnp.concatenate([rim_values, values], axis=0)
    key_features = jnp.dot(keys, key_map, preferred_element_type=jnp.float32).astype(jnp.bfloat16)
    query_features = jnp.einsum(
        "thd,hdf->thf", queries, query_maps, preferred_element_type=jnp.float32
    ).astype(jnp.bfloat16)
    block_states = jnp.einsum(
        "bwf,bwd->bfd",
        key_features.reshape(block_count, W, head_dim),
        values.reshape(block_count, W, head_dim),
        preferred_element_type=jnp.float32,
    )
    running = jnp.cumsum(block_states, axis=0)
    local_sum = running[-1]
    within_device = jnp.concatenate([jnp.zeros_like(block_states[:1]), running[:-1]], axis=0)
    zero_state = jnp.zeros((head_dim, head_dim), jnp.float32)

    def combine_states(earlier, later):
        return earlier + later

    prefix = carried_in(local_sum, "seq", combine_states, zero_state)
    starts = prefix[None] + within_device
    tensors = (
        queries,
        keys_ext,
        values_ext,
        query_features,
        key_features,
        values,
        linear_cotangent,
    )
    position_base = seq_rank * tokens_here

    def one_block(block_item):
        return window_block(block_item[0], block_item[1], tensors, position_base)

    soft_parts, linear_parts, gradient_parts = lax.map(
        one_block, (jnp.arange(block_count, dtype=jnp.int32), starts)
    )
    softmax_out = soft_parts.reshape(tokens_here, heads_here, head_dim)
    linear_out = linear_parts.reshape(tokens_here, heads_here, head_dim)
    feature_gradient = gradient_parts.reshape(tokens_here, heads_here, head_dim)
    map_gradient = lax.psum_scatter(
        jnp.einsum("the,thf->ehf", queries, feature_gradient, preferred_element_type=jnp.float32),
        "seq",
        scatter_dimension=0,
        tiled=True,
    )
    return (softmax_out, linear_out, map_gradient)


def solution(mesh):
    return jax.shard_map(
        per_device,
        mesh=mesh,
        in_specs=(
            P(("groups", "seq"), ("head", "rep"), None),
            P(("groups", "seq"), None),
            P(("groups", "seq"), None),
            P(("groups", "head", "rep"), None, None),
            P("groups", None),
            P(("groups", "seq"), ("head", "rep"), None),
        ),
        out_specs=(
            P(("groups", "seq"), ("head", "rep"), None),
            P(("groups", "seq"), ("head", "rep"), None),
            P(("groups", "seq"), ("head", "rep"), None),
        ),
        check_vma=False,
    )
```

profile of v0, /device:TPU:0, one launch (start us, length us, event | category | flops | bytes accessed | tf_op | source)
XLA Modules:
  0.0 301.4 jit_solution(11189853293392144105)
XLA Ops:
  8.8 4.9 %collective-permute-start = (bf16[512,128]{0,1:T(8,128)(2,1)S(1)}, bf16[512,128]{0,1:T(8,128)(2,1)S(1)}, u32[]{:S(2)}, u32[]{:S(2)}) collective-permute-start(bf16[512,128]{0,1:T(8,128)(2,1)S(1)} %slice.16), channel_id=1, source_target_pairs={{0,4},{4,8},{8,12},{1,5},{5,9},{9,13},{2,6},{6,10},{10,14},{3,7},{... | collective-permute-start | bytes 393224 | tf_op jit(solution)/shard_map/ppermute | solution.py:12
  14.7 3.5 %collective-permute-start.1 = (bf16[512,128]{1,0:T(8,128)(2,1)S(1)}, bf16[512,128]{1,0:T(8,128)(2,1)S(1)}, u32[]{:S(2)}, u32[]{:S(2)}) collective-permute-start(bf16[512,128]{1,0:T(8,128)(2,1)S(1)} %slice.13), channel_id=1, source_target_pairs={{0,4},{4,8},{8,12},{1,5},{5,9},{9,13},{2,6},{6,10},{10,14},{3,7},{... | collective-permute-start | bytes 393224 | tf_op jit(solution)/shard_map/ppermute | solution.py:12
  21.4 14.4 %all_gather.3 = f32[4,128,128]{2,1,0:T(8,128)S(1)} all-gather(f32[1,128,128]{2,1,0:T(8,128)S(1)} %slice.17), channel_id=1, replica_groups=mesh['groups'=2,'seq'=4,'head'=2,'rep'=2] {'seq'}, dimensions={0}, use_global_device_ids=true | all-gather | bytes 327680 | tf_op jit(solution)/shard_map/all_gather | solution.py:17
  36.0 4.8 %copy.57 = bf16[4096,4,128]{2,0,1:T(8,128)(2,1)} copy(bf16[4096,4,128]{2,1,0:T(4,128)(2,1)} %param.10) | data formatting | bytes 8388608 | tf_op jit(solution)/shard_map/while | solution.py:128
  40.8 3.2 %fusion.82 = bf16[4096,4,128]{0,2,1:T(8,128)(2,1)} fusion(bf16[4,128,128]{2,1,0:T(8,128)(2,1)S(1)} %copy-done, bf16[4096,4,128]{2,1,0:T(4,128)(2,1)S(1)} %copy-done.1), kind=kOutput, calls=%fused_computation.81 | convolution fusion | flops 538968064 | bytes 8519680 | tf_op jit(solution)/shard_map/thd,hdf->thf/dot_general | solution.py:95
  47.1 205.7 %while.30 = (s32[]{:T(128)}, bf16[8,512,4,128]{3,2,1,0:T(4,128)(2,1)}, bf16[8,512,4,128]{3,2,1,0:T(4,128)(2,1)}, bf16[8,512,4,128]{3,1,0,2:T(8,128)(2,1)}, s32[8...) while((s32[]{:T(128)}, ...), condition=%wide.region_6.7_spmd, body=%wide.region_3.6_spmd.sunk | while | flops 2974291968 | bytes 35562308 | solution.py:128
  49.3 7.5 %fusion.139 = (f32[4,512]{1,0:T(4,128)S(1)}, f32[4,512,1024]{1,2,0:T(8,128)}) fusion(pred[512,1024]{0,1:T(8,128)(4,1)S(1)} %fusion.138, bf16[4096,4,128]{2,0,1:T(8,128)(2,1)} %get-tuple-element.548, s32[]{:T(128)S(6)} %select_n.112, bf16[4608,128]{1,0:T(8,128)(2,1)} %get-tuple-element.547, s32[]{:T(128)S(6)} %select_n.113), kind=kOutput, calls=%fused_computation.90.clone.1 | convolution fusion | flops 545260544 | bytes 9707528 | tf_op jit(solution)/shard_map/while/body/eval_jaxpr/sub | solution.py:45
  56.8 4.2 %fusion.140 = bf16[1,512,4,128]{1,3,2,0:T(8,128)(2,1)S(1)} fusion(f32[4,512,1024]{1,2,0:T(8,128)} %get-tuple-element.474, f32[4,512]{1,0:T(4,128)S(1)} %get-tuple-element.475, bf16[4608,128]{0,1:T(8,128)(2,1)} %get-tuple-element.545, s32[]{:T(128)S(6)} %select_n.113), kind=kOutput, calls=%fused_computation.30.clone.1 | convolution fusion | flops 541327360 | bytes 9183236 | tf_op jit(solution)/shard_map/while/body/eval_jaxpr/hwk,kd->whd/dot_general | solution.py:47
  75.0 7.5 %fusion.139 = (f32[4,512]{1,0:T(4,128)S(1)}, f32[4,512,1024]{1,2,0:T(8,128)}) fusion(pred[512,1024]{0,1:T(8,128)(4,1)S(1)} %fusion.138, bf16[4096,4,128]{2,0,1:T(8,128)(2,1)} %get-tuple-element.548, s32[]{:T(128)S(6)} %select_n.112, bf16[4608,128]{1,0:T(8,128)(2,1)} %get-tuple-element.547, s32[]{:T(128)S(6)} %select_n.113), kind=kOutput, calls=%fused_computation.90.clone.1 | convolution fusion | flops 545260544 | bytes 9707528 | tf_op jit(solution)/shard_map/while/body/eval_jaxpr/sub | solution.py:45
  82.5 4.2 %fusion.140 = bf16[1,512,4,128]{1,3,2,0:T(8,128)(2,1)S(1)} fusion(f32[4,512,1024]{1,2,0:T(8,128)} %get-tuple-element.474, f32[4,512]{1,0:T(4,128)S(1)} %get-tuple-element.475, bf16[4608,128]{0,1:T(8,128)(2,1)} %get-tuple-element.545, s32[]{:T(128)S(6)} %select_n.113), kind=kOutput, calls=%fused_computation.30.clone.1 | convolution fusion | flops 541327360 | bytes 9183236 | tf_op jit(solution)/shard_map/while/body/eval_jaxpr/hwk,kd->whd/dot_general | solution.py:47
  100.7 7.5 %fusion.139 = (f32[4,512]{1,0:T(4,128)S(1)}, f32[4,512,1024]{1,2,0:T(8,128)}) fusion(pred[512,1024]{0,1:T(8,128)(4,1)S(1)} %fusion.138, bf16[4096,4,128]{2,0,1:T(8,128)(2,1)} %get-tuple-element.548, s32[]{:T(128)S(6)} %select_n.112, bf16[4608,128]{1,0:T(8,128)(2,1)} %get-tuple-element.547, s32[]{:T(128)S(6)} %select_n.113), kind=kOutput, calls=%fused_computation.90.clone.1 | convolution fusion | flops 545260544 | bytes 9707528 | tf_op jit(solution)/shard_map/while/body/eval_jaxpr/sub | solution.py:45
  108.2 4.2 %fusion.140 = bf16[1,512,4,128]{1,3,2,0:T(8,128)(2,1)S(1)} fusion(f32[4,512,1024]{1,2,0:T(8,128)} %get-tuple-element.474, f32[4,512]{1,0:T(4,128)S(1)} %get-tuple-element.475, bf16[4608,128]{0,1:T(8,128)(2,1)} %get-tuple-element.545, s32[]{:T(128)S(6)} %select_n.113), kind=kOutput, calls=%fused_computation.30.clone.1 | convolution fusion | flops 541327360 | bytes 9183236 | tf_op jit(solution)/shard_map/while/body/eval_jaxpr/hwk,kd->whd/dot_general | solution.py:47
  126.5 7.5 %fusion.139 = (f32[4,512]{1,0:T(4,128)S(1)}, f32[4,512,1024]{1,2,0:T(8,128)}) fusion(pred[512,1024]{0,1:T(8,128)(4,1)S(1)} %fusion.138, bf16[4096,4,128]{2,0,1:T(8,128)(2,1)} %get-tuple-element.548, s32[]{:T(128)S(6)} %select_n.112, bf16[4608,128]{1,0:T(8,128)(2,1)} %get-tuple-element.547, s32[]{:T(128)S(6)} %select_n.113), kind=kOutput, calls=%fused_computation.90.clone.1 | convolution fusion | flops 545260544 | bytes 9707528 | tf_op jit(solution)/shard_map/while/body/eval_jaxpr/sub | solution.py:45
  133.9 4.2 %fusion.140 = bf16[1,512,4,128]{1,3,2,0:T(8,128)(2,1)S(1)} fusion(f32[4,512,1024]{1,2,0:T(8,128)} %get-tuple-element.474, f32[4,512]{1,0:T(4,128)S(1)} %get-tuple-element.475, bf16[4608,128]{0,1:T(8,128)(2,1)} %get-tuple-element.545, s32[]{:T(128)S(6)} %select_n.113), kind=kOutput, calls=%fused_computation.30.clone.1 | convolution fusion | flops 541327360 | bytes 9183236 | tf_op jit(solution)/shard_map/while/body/eval_jaxpr/hwk,kd->whd/dot_general | solution.py:47
  152.2 7.5 %fusion.139 = (f32[4,512]{1,0:T(4,128)S(1)}, f32[4,512,1024]{1,2,0:T(8,128)}) fusion(pred[512,1024]{0,1:T(8,128)(4,1)S(1)} %fusion.138, bf16[4096,4,128]{2,0,1:T(8,128)(2,1)} %get-tuple-element.548, s32[]{:T(128)S(6)} %select_n.112, bf16[4608,128]{1,0:T(8,128)(2,1)} %get-tuple-element.547, s32[]{:T(128)S(6)} %select_n.113), kind=kOutput, calls=%fused_computation.90.clone.1 | convolution fusion | flops 545260544 | bytes 9707528 | tf_op jit(solution)/shard_map/while/body/eval_jaxpr/sub | solution.py:45
  159.6 4.2 %fusion.140 = bf16[1,512,4,128]{1,3,2,0:T(8,128)(2,1)S(1)} fusion(f32[4,512,1024]{1,2,0:T(8,128)} %get-tuple-element.474, f32[4,512]{1,0:T(4,128)S(1)} %get-tuple-element.475, bf16[4608,128]{0,1:T(8,128)(2,1)} %get-tuple-element.545, s32[]{:T(128)S(6)} %select_n.113), kind=kOutput, calls=%fused_computation.30.clone.1 | convolution fusion | flops 541327360 | bytes 9183236 | tf_op jit(solution)/shard_map/while/body/eval_jaxpr/hwk,kd->whd/dot_general | solution.py:47
  177.9 7.5 %fusion.139 = (f32[4,512]{1,0:T(4,128)S(1)}, f32[4,512,1024]{1,2,0:T(8,128)}) fusion(pred[512,1024]{0,1:T(8,128)(4,1)S(1)} %fusion.138, bf16[4096,4,128]{2,0,1:T(8,128)(2,1)} %get-tuple-element.548, s32[]{:T(128)S(6)} %select_n.112, bf16[4608,128]{1,0:T(8,128)(2,1)} %get-tuple-element.547, s32[]{:T(128)S(6)} %select_n.113), kind=kOutput, calls=%fused_computation.90.clone.1 | convolution fusion | flops 545260544 | bytes 9707528 | tf_op jit(solution)/shard_map/while/body/eval_jaxpr/sub | solution.py:45
  185.3 4.2 %fusion.140 = bf16[1,512,4,128]{1,3,2,0:T(8,128)(2,1)S(1)} fusion(f32[4,512,1024]{1,2,0:T(8,128)} %get-tuple-element.474, f32[4,512]{1,0:T(4,128)S(1)} %get-tuple-element.475, bf16[4608,128]{0,1:T(8,128)(2,1)} %get-tuple-element.545, s32[]{:T(128)S(6)} %select_n.113), kind=kOutput, calls=%fused_computation.30.clone.1 | convolution fusion | flops 541327360 | bytes 9183236 | tf_op jit(solution)/shard_map/while/body/eval_jaxpr/hwk,kd->whd/dot_general | solution.py:47
  203.6 7.5 %fusion.139 = (f32[4,512]{1,0:T(4,128)S(1)}, f32[4,512,1024]{1,2,0:T(8,128)}) fusion(pred[512,1024]{0,1:T(8,128)(4,1)S(1)} %fusion.138, bf16[4096,4,128]{2,0,1:T(8,128)(2,1)} %get-tuple-element.548, s32[]{:T(128)S(6)} %select_n.112, bf16[4608,128]{1,0:T(8,128)(2,1)} %get-tuple-element.547, s32[]{:T(128)S(6)} %select_n.113), kind=kOutput, calls=%fused_computation.90.clone.1 | convolution fusion | flops 545260544 | bytes 9707528 | tf_op jit(solution)/shard_map/while/body/eval_jaxpr/sub | solution.py:45
  211.0 4.2 %fusion.140 = bf16[1,512,4,128]{1,3,2,0:T(8,128)(2,1)S(1)} fusion(f32[4,512,1024]{1,2,0:T(8,128)} %get-tuple-element.474, f32[4,512]{1,0:T(4,128)S(1)} %get-tuple-element.475, bf16[4608,128]{0,1:T(8,128)(2,1)} %get-tuple-element.545, s32[]{:T(128)S(6)} %select_n.113), kind=kOutput, calls=%fused_computation.30.clone.1 | convolution fusion | flops 541327360 | bytes 9183236 | tf_op jit(solution)/shard_map/while/body/eval_jaxpr/hwk,kd->whd/dot_general | solution.py:47
  229.3 7.5 %fusion.139 = (f32[4,512]{1,0:T(4,128)S(1)}, f32[4,512,1024]{1,2,0:T(8,128)}) fusion(pred[512,1024]{0,1:T(8,128)(4,1)S(1)} %fusion.138, bf16[4096,4,128]{2,0,1:T(8,128)(2,1)} %get-tuple-element.548, s32[]{:T(128)S(6)} %select_n.112, bf16[4608,128]{1,0:T(8,128)(2,1)} %get-tuple-element.547, s32[]{:T(128)S(6)} %select_n.113), kind=kOutput, calls=%fused_computation.90.clone.1 | convolution fusion | flops 545260544 | bytes 9707528 | tf_op jit(solution)/shard_map/while/body/eval_jaxpr/sub | solution.py:45
  236.7 4.2 %fusion.140 = bf16[1,512,4,128]{1,3,2,0:T(8,128)(2,1)S(1)} fusion(f32[4,512,1024]{1,2,0:T(8,128)} %get-tuple-element.474, f32[4,512]{1,0:T(4,128)S(1)} %get-tuple-element.475, bf16[4608,128]{0,1:T(8,128)(2,1)} %get-tuple-element.545, s32[]{:T(128)S(6)} %select_n.113), kind=kOutput, calls=%fused_computation.30.clone.1 | convolution fusion | flops 541327360 | bytes 9183236 | tf_op jit(solution)/shard_map/while/body/eval_jaxpr/hwk,kd->whd/dot_general | solution.py:47
  252.8 5.2 %convolution_bitcast_fusion = f32[128,4,128]{0,2,1:T(8,128)S(1)} fusion(bf16[4096,4,128]{2,0,1:T(8,128)(2,1)} %bitcast.165, bf16[4096,4,128]{2,1,0:T(4,128)(2,1)} %param.10), kind=kOutput, calls=%fused_computation.85 | convolution fusion | flops 536870912 | bytes 8650752 | tf_op jit(solution)/shard_map/the,thf->ehf/dot_general | solution.py:135
  260.1 33.0 %all-reduce.4.cloned.1.call-done = f32[128,4,128]{2,1,0:T(4,128)} async-done(((f32[128,4,128]{2,1,0:T(4,128)}), f32[128,4,128]{2,1,0:T(4,128)}) %all-reduce.4.cloned.1.call-update) | async-done | bytes 262160
  (176 shorter events, 118.2 us)
Async XLA Ops:
  7.2 33.6 %copy-start = (bf16[4,128,128]{2,1,0:T(8,128)(2,1)S(1)}, bf16[4,128,128]{2,1,0:T(8,128)(2,1)}, u32[]{:S(2)}) copy-start(bf16[4,128,128]{2,1,0:T(8,128)(2,1)} %param.13) | copy-start | bytes 393220
  7.2 12.7 %copy-start.3 = (bf16[4096,128]{1,0:T(8,128)(2,1)S(1)}, bf16[4096,128]{1,0:T(8,128)(2,1)}, u32[]{:S(2)}) copy-start(bf16[4096,128]{1,0:T(8,128)(2,1)} %param.12) | copy-start | bytes 3145732
  7.2 285.9 %all-reduce.4.cloned.1.call-start = ((), (), s32[]{:S(2)}) async-start(), calls=%async_computation | async-start | bytes 524288
  8.8 36.0 %collective-permute-start = (bf16[512,128]{0,1:T(8,128)(2,1)S(1)}, bf16[512,128]{0,1:T(8,128)(2,1)S(1)}, u32[]{:S(2)}, u32[]{:S(2)}) collective-permute-start(bf16[512,128]{0,1:T(8,128)(2,1)S(1)} %slice.16), channel_id=1, source_target_pairs={{0,4},{4,8},{8,12},{1,5},{5,9},{9,13},{2,6},{6,10},{10,14},{3,7},{... | collective-permute-start | bytes 393224 | tf_op jit(solution)/shard_map/ppermute | solution.py:12
  14.7 31.3 %collective-permute-start.1 = (bf16[512,128]{1,0:T(8,128)(2,1)S(1)}, bf16[512,128]{1,0:T(8,128)(2,1)S(1)}, u32[]{:S(2)}, u32[]{:S(2)}) collective-permute-start(bf16[512,128]{1,0:T(8,128)(2,1)S(1)} %slice.13), channel_id=1, source_target_pairs={{0,4},{4,8},{8,12},{1,5},{5,9},{9,13},{2,6},{6,10},{10,14},{3,7},{... | collective-permute-start | bytes 393224 | tf_op jit(solution)/shard_map/ppermute | solution.py:12
  19.9 1.0 copy-start.4
  36.0 4.8 %copy-start.1 = (bf16[4096,4,128]{2,1,0:T(4,128)(2,1)S(1)}, bf16[4096,4,128]{2,1,0:T(4,128)(2,1)}, u32[]{:S(2)}) copy-start(bf16[4096,4,128]{2,1,0:T(4,128)(2,1)} %param.10) | copy-start | bytes 12582916
  40.8 5.2 %copy-start.2 = (bf16[4096,128]{1,0:T(8,128)(2,1)S(1)}, bf16[4096,128]{1,0:T(8,128)(2,1)}, u32[]{:S(2)}) copy-start(bf16[4096,128]{1,0:T(8,128)(2,1)} %param.11) | copy-start | bytes 3145732
  252.8 6.0 %copy-start.5 = (u32[32]{0:T(128)S(1)}, u32[32]{0:T(128)}, u32[]{:S(2)}) copy-start(u32[32]{0:T(128)} %constant.109) | copy-start | bytes 388
Sparse Core Ops, SparseCore 0:
  258.9 34.1 all-reduce.3
where the time goes:
time: 303 us; the launch traced here: 301 us
  matrix products  163 us (54%)
  local copies, waits for them, and re-layouts  50.4 us (17%)
  waiting for transfers between devices  33.1 us (11%)
  between operations  14.9 us (5%)
  blocking collectives  14.4 us (5%)
  other arithmetic  11.6 us (4%)
  starting transfers between devices  8.46 us (3%)
  loops' own time  5.98 us (2%)
    sub x8, matrix products, window_block(): shifted_exp = jnp.exp(scores - highest)  59.7 us
    dot_general x8, matrix products, window_block(): jnp.einsum('hwk,kd->whd', weights, value_window, preferred_element_type=j...  33.7 us
    unnamed x2, waiting for transfers between devices  33.1 us
    dynamic_update_slice x40, local copies, waits for them, and re-layouts, per_device(): lax.map(one_block, (jnp.arange(block_count, dtype=jnp.int32), starts))  25 us
    dot_general x8, matrix products, window_block(): jnp.einsum('hws,sd->whd', linear_scores, value_block, preferred_element_t...  17.5 us
    dot_general x8, matrix products, window_block(): jnp.einsum('hws,sf->whf', back_scores, key_block, preferred_element_type=...  16.1 us
    all_gather x1, blocking collectives, carried_in(): everything = lax.all_gather(array, axis)  14.4 us
    dot_general x8, matrix products, window_block(): jnp.einsum('whf,fd->whd', feature_block.astype(jnp.float32), start_state,...  13.8 us
  transfers between devices with their start and end apart: 3, of which 1 were waited for; matrix products, arithmetic and copies ran while one was open for 5% of the time, Pallas kernels for 0%

commit v1 on v0

v1 whole, which is shorter than its diff:
```python
import functools

import jax
import jax.numpy as jnp
import numpy as np
from jax import lax
from jax.experimental import pallas as pl
from jax.experimental.pallas import tpu as pltpu
from jax.sharding import PartitionSpec as P

W = 512
TILE = 128
BF = jnp.bfloat16
F32 = jnp.float32
LOG2E = 1.4426950408889634
VMEM_LIMIT = 56 * 2**20


def dot_nn(a, b):
    return jnp.dot(a, b, preferred_element_type=F32)


def dot_nt(a, b):
    return lax.dot_general(a, b, (((1,), (1,)), ((), ())), preferred_element_type=F32)


def dot_tn(a, b):
    return lax.dot_general(a, b, (((0,), (0,)), ((), ())), preferred_element_type=F32)


def tokens_of_rows(rows, heads):
    return lax.broadcasted_iota(jnp.int32, (rows, TILE), 0) // heads


def padded16(rows):
    return -(-rows // 16) * 16


def backward_kernel(
    heads, ranks, slab, q_ref, c_ref, k_ref, v_ref, map_ref, send_ref, rim_ref, acc, state, qs, cs, fs, gi, qi
):
    step, steps = pl.program_id(0), pl.num_programs(0)
    head_dim = map_ref.shape[0]
    tiles = k_ref.shape[0] // TILE
    rows = TILE * heads

    @pl.when(step == 0)
    def _():
        acc[...] = jnp.zeros_like(acc)
        state[...] = jnp.zeros_like(state)

    first = lax.axis_index("seq") * (steps * tiles * TILE) + step * (tiles * TILE)
    tok = tokens_of_rows(rows, heads)
    causal = lax.broadcasted_iota(jnp.int32, (rows, TILE), 1) <= tok
    key_features = dot_nn(k_ref[...], map_ref[...]).astype(BF)
    carried = state[...]
    for t in range(tiles):
        sl, tl = slice(t * rows, (t + 1) * rows), slice(t * TILE, (t + 1) * TILE)
        cot, val, kf = c_ref[sl, :], v_ref[tl, :], key_features[tl, :]
        back = jnp.where(causal, dot_nt(cot, val), 0.0).astype(BF)
        fs[sl, :] = dot_nn(
            jnp.concatenate([back, cot], 1), jnp.concatenate([kf, carried.astype(BF)], 0)
        )
        factor = lax.rsqrt((tok + (first + t * TILE + 1)).astype(F32))
        qs[sl, :] = q_ref[sl, :].astype(F32) * factor
        cs[sl, :] = cot.astype(F32)
        carried = carried + dot_tn(val, kf)
    state[...] = carried
    for h in range(heads):
        pick = pl.ds(h, tiles * TILE, stride=heads)
        right = jnp.concatenate([fs[pick, :].astype(BF), cs[pick, :].astype(BF)], 1)
        acc[h] += dot_tn(qs[pick, :].astype(BF), right)

    @pl.when(step == steps - 1)
    def _():
        for h in range(heads):
            pick = pl.ds(h, head_dim, stride=heads)
            gi[pick, :] = acc[h, :, :head_dim]
            qi[pick, :] = acc[h, :, head_dim:]
        total = state[...]
        high = total.astype(BF)
        low = (total - high.astype(F32)).astype(BF)
        for d in range(ranks):
            send_ref[d, :head_dim, :] = jnp.concatenate([high, low], 1)
            part = jnp.concatenate(
                [gi[d * slab : (d + 1) * slab, :], qi[d * slab : (d + 1) * slab, :]], 1
            )
            spare = padded16(slab) - slab
            if spare:
                part = jnp.concatenate([part, jnp.zeros((spare, 2 * head_dim), F32)], 0)
            send_ref[d, head_dim:, :] = part.astype(BF)
        rim_ref[:W, :] = k_ref[...][-W:, :]
        rim_ref[W:, :] = v_ref[...][-W:, :]


def soft_block(heads, q_ref, keys_before, keys_here, values_before, values_here, o_ref, before_ok):
    head_dim = q_ref.shape[1]
    scale = float(LOG2E / np.sqrt(head_dim))
    rows = TILE * heads
    low = lax.broadcasted_iota(jnp.int32, (rows, TILE), 1) <= tokens_of_rows(rows, heads)
    for t in range(W // TILE):
        sl = slice(t * rows, (t + 1) * rows)
        start, end = t * TILE, (t + 1) * TILE
        keys = jnp.concatenate([keys_before[start:, :], keys_here[:end, :]], 0)
        values = jnp.concatenate([values_before[start:, :], values_here[:end, :]], 0)
        scores = dot_nt(q_ref[sl, :], keys)
        parts = [scores[:, j * TILE : (j + 1) * TILE] for j in range(W // TILE + 1)]
        parts[0] = jnp.where(low, -1e30, parts[0])
        parts[-1] = jnp.where(low, parts[-1], -1e30)
        if before_ok is not None:
            for j in range(W // TILE - t):
                parts[j] = jnp.where(before_ok, parts[j], -1e30)
        highest = jnp.max(functools.reduce(jnp.maximum, parts), axis=1, keepdims=True)
        weights = jnp.concatenate(
            [jnp.exp2((part - highest) * scale).astype(BF) for part in parts], 1
        )
        both = dot_nn(weights, jnp.concatenate([values, jnp.ones_like(values)], 1))
        o_ref[sl, :] = (both[:, :head_dim] / both[:, head_dim:]).astype(BF)


def softmax_kernel(heads, q_ref, kb_ref, kh_ref, vb_ref, vh_ref, o_ref):
    soft_block(heads, q_ref, kb_ref, kh_ref, vb_ref, vh_ref, o_ref, None)


def forward_kernel(
    heads, ranks, slab, q_ref, k_ref, v_ref, map_ref, qmap_ref, got_ref, rim_ref, _, o_ref, soft_ref, grad_ref, state, qs, os
):
    step, steps = pl.program_id(0), pl.num_programs(0)
    head_dim = map_ref.shape[0]
    tiles = k_ref.shape[0] // TILE
    rows = TILE * heads
    rank = lax.axis_index("seq")

    @pl.when(step == 0)
    def _():
        before = jnp.zeros((head_dim, head_dim), F32)
        mine = before
        grad = jnp.zeros((slab, head_dim), F32)
        for r in range(ranks):
            mine = jnp.where(rank == r, before, mine)
            part = got_ref[r, head_dim:, :][:slab]
            if r:
                high = before.astype(BF)
                low = (before - high.astype(F32)).astype(BF)
                grad = grad + dot_nn(part[:, head_dim:], high) + dot_nn(part[:, head_dim:], low)
            grad = grad + part[:, :head_dim].astype(F32)
            states = got_ref[r, :head_dim, :].astype(F32)
            before = before + (states[:, :head_dim] + states[:, head_dim:])
        grad_ref[...] = grad
        state[...] = mine.T
        soft_block(
            heads, q_ref, rim_ref.at[:W], k_ref, rim_ref.at[W:], v_ref, soft_ref, rank > 0
        )

    first = rank * (steps * tiles * TILE) + step * (tiles * TILE)
    qs[...] = q_ref[...].astype(F32)
    key_features = dot_nn(k_ref[...], map_ref[...]).astype(BF)
    features = [
        dot_nn(qs[pl.ds(h, tiles * TILE, stride=heads), :].astype(BF), qmap_ref[h]).astype(BF)
        for h in range(heads)
    ]
    tok = lax.broadcasted_iota(jnp.int32, (TILE, TILE), 0)
    causal = jnp.concatenate([lax.broadcasted_iota(jnp.int32, (TILE, TILE), 1) <= tok] * heads, 0)
    carried = state[...]
    for t in range(tiles):
        tl = slice(t * TILE, (t + 1) * TILE)
        val, kf = v_ref[tl, :], key_features[tl, :]
        qf = jnp.concatenate([x[tl, :] for x in features], 0)
        inner = jnp.where(causal, dot_nt(qf, kf), 0.0).astype(BF)
        out = dot_nn(
            jnp.concatenate([inner, qf], 1), jnp.concatenate([val, carried.astype(BF)], 0)
        )
        factor = lax.rsqrt((tok + (first + t * TILE + 1)).astype(F32))
        for h in range(heads):
            os[pl.ds(t * rows + h, TILE, stride=heads), :] = out[h * TILE : (h + 1) * TILE, :] * factor
        carried = carried + dot_tn(kf, val)
    state[...] = carried
    o_ref[...] = os[...].astype(BF)


def per_device(ranks, queries, keys, values, query_maps, key_map, linear_cotangent):
    tokens, heads, head_dim = queries.shape
    blocks = tokens // W
    block_rows = W * heads
    slab = head_dim // ranks * heads
    params = pltpu.CompilerParams(vmem_limit_bytes=VMEM_LIMIT)
    q_rows = queries.reshape(tokens * heads, head_dim)
    c_rows = linear_cotangent.reshape(tokens * heads, head_dim)
    row_spec = pl.BlockSpec((block_rows, head_dim), lambda i: (i, 0))
    key_spec = pl.BlockSpec((W, head_dim), lambda i: (i, 0))

    def whole(shape):
        return pl.BlockSpec(shape, lambda i: (0,) * len(shape))

    packet = (ranks, head_dim + padded16(slab), 2 * head_dim)
    send, rim = pl.pallas_call(
        functools.partial(backward_kernel, heads, ranks, slab),
        grid=(blocks,),
        in_specs=[row_spec, row_spec, key_spec, key_spec, whole(key_map.shape)],
        out_specs=[whole(packet), whole((2 * W, head_dim))],
        out_shape=[
            jax.ShapeDtypeStruct(packet, BF),
            jax.ShapeDtypeStruct((2 * W, head_dim), BF),
        ],
        scratch_shapes=[
            pltpu.VMEM((heads, head_dim, 2 * head_dim), F32),
            pltpu.VMEM((head_dim, head_dim), F32),
            pltpu.VMEM((block_rows, head_dim), F32),
            pltpu.VMEM((block_rows, head_dim), F32),
            pltpu.VMEM((block_rows, head_dim), F32),
            pltpu.VMEM((heads * head_dim, head_dim), F32),
            pltpu.VMEM((heads * head_dim, head_dim), F32),
        ],
        compiler_params=params,
        name="backward",
    )(q_rows, c_rows, keys, values, key_map)

    got = lax.all_to_all(send, "seq", 0, 0)
    rim = lax.ppermute(rim, "seq", [(r, r + 1) for r in range(ranks - 1)])

    later_rows = pl.BlockSpec((block_rows, head_dim), lambda i: (i + 1, 0))
    later_keys = pl.BlockSpec((W, head_dim), lambda i: (i + 1, 0))
    soft_rows = pl.pallas_call(
        functools.partial(softmax_kernel, heads),
        grid=(blocks - 1,),
        in_specs=[later_rows, key_spec, later_keys, key_spec, later_keys],
        out_specs=later_rows,
        out_shape=jax.ShapeDtypeStruct(q_rows.shape, BF),
        compiler_params=params,
        name="softmax",
    )(q_rows, keys, keys, values, values)

    linear_rows, soft_rows, gradient = pl.pallas_call(
        functools.partial(forward_kernel, heads, ranks, slab),
        grid=(blocks,),
        in_specs=[
            row_spec,
            key_spec,
            key_spec,
            whole(key_map.shape),
            whole(query_maps.shape),
            whole(packet),
            whole((2 * W, head_dim)),
            pl.BlockSpec(memory_space=pl.ANY),
        ],
        out_specs=[row_spec, whole((block_rows, head_dim)), whole((slab, head_dim))],
        out_shape=[
            jax.ShapeDtypeStruct(q_rows.shape, BF),
            jax.ShapeDtypeStruct(q_rows.shape, BF),
            jax.ShapeDtypeStruct((slab, head_dim), F32),
        ],
        scratch_shapes=[
            pltpu.VMEM((head_dim, head_dim), F32),
            pltpu.VMEM((block_rows, head_dim), F32),
            pltpu.VMEM((block_rows, head_dim), F32),
        ],
        input_output_aliases={7: 1},
        compiler_params=params,
        name="forward",
    )(q_rows, keys, values, key_map, query_maps, got, rim, soft_rows)

    return (
        soft_rows.reshape(queries.shape),
        linear_rows.reshape(queries.shape),
        gradient.reshape(head_dim // ranks, heads, head_dim),
    )


def solution(mesh):
    return jax.shard_map(
        functools.partial(per_device, mesh.shape["seq"]),
        mesh=mesh,
        in_specs=(
            P(("groups", "seq"), ("head", "rep"), None),
            P(("groups", "seq"), None),
            P(("groups", "seq"), None),
            P(("groups", "head", "rep"), None, None),
            P("groups", None),
            P(("groups", "seq"), ("head", "rep"), None),
        ),
        out_specs=(
            P(("groups", "seq"), ("head", "rep"), None),
            P(("groups", "seq"), ("head", "rep"), None),
            P(("groups", "seq"), ("head", "rep"), None),
        ),
        check_vma=False,
    )
```

time: 303 us -> 59.4 us (0.20)
  matrix products: 163 us -> 0 us
  local copies, waits for them, and re-layouts: 50.4 us -> 1.48 us
  Pallas kernels: 0 us -> 46.5 us
  waiting for transfers between devices: 33.1 us -> 0.01 us
  blocking collectives: 14.4 us -> 0 us
  between operations: 14.9 us -> 0.65 us
  other arithmetic: 11.6 us -> 0 us
  loops' own time: 5.98 us -> 0 us
    dot_general x44 -> x0, matrix products: 103 us -> none  [the longest x8 33.7 us: window_block(): jnp.einsum('hwk,kd->whd', weights, value_window, preferred_element_type=j...]
    sub x8 -> x0, matrix products: 59.7 us -> none  [window_block(): shifted_exp = jnp.exp(scores - highest)]
    pallas_call x0 -> x3, Pallas kernels: none -> 46.5 us  [the longest x1 18.7 us: per_device(): pl.pallas_call(functools.partial(softmax_kernel, heads), grid=(blocks - 1...]
    unnamed x2 -> x0, waiting for transfers between devices: 33.1 us -> none
    dynamic_update_slice x40 -> x0, local copies, waits for them, and re-layouts: 25 us -> none  [per_device(): lax.map(one_block, (jnp.arange(block_count, dtype=jnp.int32), starts))]
    dynamic_slice x16 -> x0, local copies, waits for them, and re-layouts: 14.7 us -> none  [the longest x8 9.78 us: window_block(): cotangent_block = lax.dynamic_slice_in_dim(cotangent, first_row, W, 0)]
    all_gather x1 -> x0, blocking collectives: 14.4 us -> none  [carried_in(): everything = lax.all_gather(array, axis)]
    and x8 -> x0, other arithmetic: 7.21 us -> none  [window_block(): allowed = (spacing >= 0) & (spacing < W) & (key_pos[None, :] >= 0)]
  transfers between devices with their start and end apart: 3 -> 2, of which waited for: 1 -> 0; matrix products, arithmetic and copies ran while one was open for 5% -> 0% of each run, Pallas kernels for 0% -> 32%
where the time goes in v1:
time: 59.4 us; the launch traced here: 58.8 us
  Pallas kernels  46.5 us (78%)
  starting transfers between devices  10.3 us (17%)
  local copies, waits for them, and re-layouts  1.48 us (2%)
  between operations  0.65 us (1%)
    pallas_call x1, Pallas kernels, per_device(): pl.pallas_call(functools.partial(softmax_kernel, heads), grid=(blocks - 1...  18.7 us
    pallas_call x1, Pallas kernels, per_device(): pl.pallas_call(functools.partial(forward_kernel, heads, ranks, slab), gri...  14.9 us
    pallas_call x1, Pallas kernels, per_device(): pl.pallas_call(functools.partial(backward_kernel, heads, ranks, slab), gr...  12.8 us
    all_to_all x1, starting transfers between devices, per_device(): got = lax.all_to_all(send, 'seq', 0, 0)  6.32 us
    ppermute x1, starting transfers between devices, per_device(): rim = lax.ppermute(rim, 'seq', [(r, r + 1) for r in range(ranks - 1)])  3.93 us
    unnamed x4, local copies, waits for them, and re-layouts  1.48 us
  transfers between devices with their start and end apart: 2, of which 0 were waited for; matrix products, arithmetic and copies ran while one was open for 0% of the time, Pallas kernels for 32%

profile of v1, /device:TPU:0, one launch (start us, length us, event | category | flops | bytes accessed | tf_op | source)
XLA Modules:
  0.0 58.8 jit_solution(1417208933648122495)
XLA Ops:
  0.6 12.8 %backward.1 = (bf16[4,256,256]{2,1,0:T(8,128)(2,1)}, bf16[1024,128]{1,0:T(8,128)(2,1)}) custom-call(bf16[16384,128]{1,0:T(8,128)(2,1)} %bitcast.5, bf16[16384,128]{1,0:T(8,128)(2,1)} %bitcast.9, bf16[4096,128]{1,0:T(8,128)(2,1)} %k_ref.3, bf16[4096,128]{1,0:T(8,128)(2,1)} %v_ref.3, bf16[128,128]{1,0:T(8,128)(2,1)} %map_ref.3), custom_call_target="tpu_custom_call" | custom-call | tf_op jit(solution)/shard_map/backward/pallas_call | solution.py:196
  13.5 6.3 %all-to-all-start = ((bf16[4,256,256]{2,1,0:T(8,128)(2,1)}), bf16[4,256,256]{2,1,0:T(8,128)(2,1)S(1)}, u32[]{:S(2)}, u32[]{:S(2)}) async-start(bf16[4,256,256]{2,1,0:T(8,128)(2,1)} %get-tuple-element.8), calls=%async_computation | async-start | bytes 1048576 | tf_op jit(solution)/shard_map/all_to_all | solution.py:218
  19.8 3.9 %collective-permute-start = (bf16[1024,128]{1,0:T(8,128)(2,1)}, bf16[1024,128]{1,0:T(8,128)(2,1)S(1)}, u32[]{:S(2)}, u32[]{:S(2)}) collective-permute-start(bf16[1024,128]{1,0:T(8,128)(2,1)} %get-tuple-element.9), channel_id=1, source_target_pairs={{0,4},{4,8},{8,12},{1,5},{5,9},{9,13},{2,6},{6,10},{10,14},{3,7},{... | collective-permute-start | bytes 786440 | tf_op jit(solution)/shard_map/ppermute | solution.py:219
  23.7 18.7 %softmax.1._ = bf16[16384,128]{1,0:T(8,128)(2,1)} custom-call(bf16[16384,128]{1,0:T(8,128)(2,1)} %bitcast.6, bf16[4096,128]{1,0:T(8,128)(2,1)} %k_ref.3, bf16[4096,128]{1,0:T(8,128)(2,1)} %k_ref.3, bf16[4096,128]{1,0:T(8,128)(2,1)} %v_ref.3, bf16[4096,128]{1,0:T(8,128)(2,1)} %v_ref.3), custom_call_target="tpu_custom_call" | custom-call | tf_op jit(solution)/shard_map/softmax/pallas_call | solution.py:223
  42.4 0.0 collective-permute-done.rim_ref
  42.4 0.0 copy-start.1
  42.4 0.0 all-to-all-done.got_ref
  42.4 0.7 %copy-done.1 = bf16[1024,128]{1,0:T(8,128)(2,1)} copy-done((bf16[1024,128]{1,0:T(8,128)(2,1)}, bf16[1024,128]{1,0:T(8,128)(2,1)S(1)}, u32[]{:S(2)}) %copy-start.1) | copy-done | bytes 262168
  43.1 0.0 copy-start
  43.1 0.8 %copy-done = bf16[4,256,256]{2,1,0:T(8,128)(2,1)} copy-done((bf16[4,256,256]{2,1,0:T(8,128)(2,1)}, bf16[4,256,256]{2,1,0:T(8,128)(2,1)S(1)}, u32[]{:S(2)}) %copy-start) | copy-done | bytes 524312
  43.9 14.9 %forward.1 = (bf16[16384,128]{1,0:T(8,128)(2,1)}, bf16[16384,128]{1,0:T(8,128)(2,1)}, f32[128,128]{1,0:T(8,128)}) custom-call(bf16[16384,128]{1,0:T(8,128)(2,1)} %bitcast.7, bf16[4096,128]{1,0:T(8,128)(2,1)} %k_ref.3, bf16[4096,128]{1,0:T(8,128)(2,1)} %v_ref.3, bf16[128,128]{1,0:T(8,128)(2,1)} %map_ref.3, ...), custom_call_target="tpu_custom_call", output_to_operand_aliasing={{1}: (7, {})} | custom-call | tf_op jit(solution)/shard_map/forward/pallas_call | solution.py:233
Async XLA Ops:
  13.5 29.0 %all-to-all-start = ((bf16[4,256,256]{2,1,0:T(8,128)(2,1)}), bf16[4,256,256]{2,1,0:T(8,128)(2,1)S(1)}, u32[]{:S(2)}, u32[]{:S(2)}) async-start(bf16[4,256,256]{2,1,0:T(8,128)(2,1)} %get-tuple-element.8), calls=%async_computation | async-start | bytes 1048576 | tf_op jit(solution)/shard_map/all_to_all | solution.py:218
  19.8 22.7 %collective-permute-start = (bf16[1024,128]{1,0:T(8,128)(2,1)}, bf16[1024,128]{1,0:T(8,128)(2,1)S(1)}, u32[]{:S(2)}, u32[]{:S(2)}) collective-permute-start(bf16[1024,128]{1,0:T(8,128)(2,1)} %get-tuple-element.9), channel_id=1, source_target_pairs={{0,4},{4,8},{8,12},{1,5},{5,9},{9,13},{2,6},{6,10},{10,14},{3,7},{... | collective-permute-start | bytes 786440 | tf_op jit(solution)/shard_map/ppermute | solution.py:219
  42.4 0.7 %copy-start.1 = (bf16[1024,128]{1,0:T(8,128)(2,1)}, bf16[1024,128]{1,0:T(8,128)(2,1)S(1)}, u32[]{:S(2)}) copy-start(bf16[1024,128]{1,0:T(8,128)(2,1)S(1)} %collective-permute-done.rim_ref) | copy-start | bytes 786436
  43.1 0.8 %copy-start = (bf16[4,256,256]{2,1,0:T(8,128)(2,1)}, bf16[4,256,256]{2,1,0:T(8,128)(2,1)S(1)}, u32[]{:S(2)}) copy-start(bf16[4,256,256]{2,1,0:T(8,128)(2,1)S(1)} %all-to-all-done.got_ref) | copy-start | bytes 1572868

commit v2 on v1

v2 whole, which is shorter than its diff:
```python
import functools

import jax
import jax.numpy as jnp
import numpy as np
from jax import lax
from jax.experimental import pallas as pl
from jax.experimental.pallas import tpu as pltpu
from jax.sharding import PartitionSpec as P

W = 512
TILE = 128
CHUNK = 1024
GROUP = 4
BF = jnp.bfloat16
F32 = jnp.float32
LOG2E = 1.4426950408889634
VMEM_LIMIT = 64 * 2**20 - 2**17


def dot_nn(a, b):
    return jnp.dot(a, b, preferred_element_type=F32)


def dot_nt(a, b):
    return lax.dot_general(a, b, (((1,), (1,)), ((), ())), preferred_element_type=F32)


def dot_tn(a, b):
    return lax.dot_general(a, b, (((0,), (0,)), ((), ())), preferred_element_type=F32)


def tokens_of_rows(rows, heads):
    return lax.broadcasted_iota(jnp.int32, (rows, TILE), 0) // heads


def padded16(rows):
    return -(-rows // 16) * 16


def staged(count, *stages):
    for x in range(count + len(stages) - 1):
        for depth in reversed(range(len(stages))):
            if 0 <= x - depth < count:
                stages[depth](x - depth)


def causal_keep(heads):
    tok = lax.broadcasted_iota(jnp.int32, (TILE, TILE), 0)
    causal = lax.broadcasted_iota(jnp.int32, (TILE, TILE), 1) <= tok
    return jnp.concatenate([jnp.where(causal, 1.0, 0.0)] * heads, 0).astype(BF)


def backward_kernel(
    heads, ranks, slab, q_ref, c_ref, k_ref, v_ref, map_ref, send_ref, rim_ref, acc, state, keep, qs, cs, gi, qi
):
    step, steps = pl.program_id(0), pl.num_programs(0)
    head_dim = map_ref.shape[0]
    tiles = k_ref.shape[0] // TILE
    rows = TILE * heads
    group = min(GROUP, tiles)

    @pl.when(step == 0)
    def _():
        acc[...] = jnp.zeros_like(acc)
        state[...] = jnp.zeros_like(state)
        keep[...] = causal_keep(heads)

    first = lax.axis_index("seq") * (steps * tiles * TILE) + step * (tiles * TILE)
    key_features = dot_nn(k_ref[...], map_ref[...]).astype(BF)
    carried = state[...]
    starts, cots, back, grads = [], {}, {}, {}
    for t in range(tiles):
        tl = slice(t * TILE, (t + 1) * TILE)
        starts.append(carried.astype(BF))
        carried = carried + dot_tn(v_ref[tl, :], key_features[tl, :])
    state[...] = carried

    def widen(t):
        sl = slice(t * rows, (t + 1) * rows)
        qs[sl, :] = q_ref[sl, :].astype(F32)
        cs[sl, :] = c_ref[sl, :].astype(F32)

    def part(ref, t, h, count=TILE):
        return ref[pl.ds(t * rows + h, count, stride=heads), :]

    def score(t):
        cots[t] = jnp.concatenate([part(cs, t, h).astype(BF) for h in range(heads)], 0)
        back[t] = dot_nt(cots[t], v_ref[t * TILE : (t + 1) * TILE, :]).astype(BF) * keep[...]

    def gradient(t):
        out = dot_nn(
            jnp.concatenate([back.pop(t), cots[t]], 1),
            jnp.concatenate([key_features[t * TILE : (t + 1) * TILE, :], starts[t]], 0),
        )
        grads[t] = out.astype(BF)

    def gather(t):
        if (t + 1) % group:
            return
        begin = t + 1 - group
        tok = lax.broadcasted_iota(jnp.int32, (group * TILE, head_dim), 0)
        factor = lax.rsqrt((tok + (first + begin * TILE + 1)).astype(F32))
        for h in range(heads):
            hs = slice(h * TILE, (h + 1) * TILE)
            right = jnp.concatenate(
                [
                    jnp.concatenate([grads[u][hs, :], cots[u][hs, :]], 1)
                    for u in range(begin, t + 1)
                ],
                0,
            )
            acc[h] += dot_tn((part(qs, begin, h, group * TILE) * factor).astype(BF), right)

    staged(tiles, widen, score, gradient, gather)

    @pl.when(step == steps - 1)
    def _():
        for h in range(heads):
            pick = pl.ds(h, head_dim, stride=heads)
            gi[pick, :] = acc[h, :, :head_dim]
            qi[pick, :] = acc[h, :, head_dim:]
        for d in range(ranks):
            send_ref[d, :head_dim, :] = state[...].astype(BF)
            for n, terms in enumerate((gi, qi)):
                part = terms[d * slab : (d + 1) * slab, :]
                spare = padded16(slab) - slab
                if spare:
                    part = jnp.concatenate([part, jnp.zeros((spare, head_dim), F32)], 0)
                begin = head_dim + n * padded16(slab)
                send_ref[d, begin : begin + padded16(slab), :] = part.astype(BF)
        rim_ref[:W, :] = k_ref[...][-W:, :]
        rim_ref[W:, :] = v_ref[...][-W:, :]


def window_biases(heads, before, after):
    rows = TILE * heads
    low = lax.broadcasted_iota(jnp.int32, (rows, TILE), 1) <= tokens_of_rows(rows, heads)
    before[...] = jnp.where(low, -1e30, 0.0)
    after[...] = jnp.where(low, 0.0, -1e30)


def soft_stages(rows, q_ref, o_ref, keys_of, values_of, before, after, extra):
    head_dim = q_ref.shape[1]
    scale = float(LOG2E / np.sqrt(head_dim))
    held = {}

    def score(t):
        held[t] = dot_nt(q_ref[t * rows : (t + 1) * rows, :], keys_of(t))

    def weigh(t):
        scores = held[t]
        parts = [scores[:, j * TILE : (j + 1) * TILE] for j in range(W // TILE + 1)]
        parts[0] = parts[0] + before[...]
        parts[-1] = parts[-1] + after[...]
        if extra is not None:
            parts = [part if j == W // TILE else part + extra(t, j) for j, part in enumerate(parts)]
        highest = jnp.max(functools.reduce(jnp.maximum, parts), axis=1, keepdims=True)
        held[t] = jnp.concatenate(
            [jnp.exp2((part - highest) * scale).astype(BF) for part in parts], 1
        )

    def combine(t):
        values = values_of(t)
        both = dot_nn(held.pop(t), jnp.concatenate([values, jnp.ones_like(values)], 1))
        o_ref[t * rows : (t + 1) * rows, :] = (both[:, :head_dim] / both[:, head_dim:]).astype(BF)

    return score, weigh, combine


def softmax_kernel(heads, q_ref, kb_ref, kh_ref, vb_ref, vh_ref, o_ref, before, after):
    @pl.when(pl.program_id(0) == 0)
    def _():
        window_biases(heads, before, after)

    def window(left, here):
        def of(t):
            start, end = t * TILE, (t + 1) * TILE
            if start >= W:
                return here[start - W : end, :]
            return jnp.concatenate([left[start:, :], here[:end, :]], 0)

        return of

    stages = soft_stages(
        TILE * heads, q_ref, o_ref, window(kb_ref, kh_ref), window(vb_ref, vh_ref), before, after, None
    )
    count = kh_ref.shape[0] // TILE
    skipped = W // TILE

    @pl.when(pl.program_id(0) == 0)
    def _():
        if count > skipped:
            staged(count - skipped, *(lambda t, stage=stage: stage(t + skipped) for stage in stages))

    @pl.when(pl.program_id(0) > 0)
    def _():
        staged(count, *stages)


def forward_kernel(
    heads, ranks, slab, soft_steps, q_ref, k_ref, v_ref, map_ref, qmap_ref, soft_q_ref, got, rim_ref, _,
    o_ref, soft_ref, grad_ref, state, keep, qs, os, keys_ext, values_ext, before, after
):
    step, steps = pl.program_id(0), pl.num_programs(0)
    head_dim = map_ref.shape[0]
    tokens = k_ref.shape[0]
    tiles = tokens // TILE
    rows = TILE * heads
    rank = lax.axis_index("seq")

    @pl.when(step == 0)
    def _():
        keys_ext[:W, :] = rim_ref[:W, :]
        values_ext[:W, :] = rim_ref[W:, :]
        keys_ext[W:, :] = k_ref[:W, :]
        values_ext[W:, :] = v_ref[:W, :]
        window_biases(heads, before, after)
        keep[...] = causal_keep(heads)
        earlier = jnp.zeros((head_dim, head_dim), F32)
        mine = earlier
        grad = jnp.zeros((slab, head_dim), F32)
        for r in range(ranks):
            mine = jnp.where(rank == r, earlier, mine)
            middle = head_dim + padded16(slab)
            grad = grad + got[r, head_dim:middle, :].astype(F32)[:slab]
            if r:
                high = earlier.astype(BF)
                low = (earlier - high.astype(F32)).astype(BF)
                products = got[r, middle:, :]
                grad = grad + (dot_nn(products, high) + dot_nn(products, low))[:slab]
            earlier = earlier + got[r, :head_dim, :].astype(F32)
        grad_ref[...] = grad
        state[...] = mine.T

    first = rank * (steps * tokens) + step * tokens
    soft_tiles = soft_q_ref.shape[0] // rows
    soft_first = jnp.minimum(step, soft_steps - 1) * soft_tiles

    def window(ref):
        def of(u):
            start = pl.multiple_of((soft_first + u) * TILE, TILE)
            return ref[pl.ds(start, W + TILE), :]

        return of

    def outside(u, j):
        early = (soft_first + u + j) * TILE < W
        return jnp.where(jnp.logical_and(rank == 0, early), -1e30, 0.0)

    soft = soft_stages(
        rows, soft_q_ref, soft_ref, window(keys_ext), window(values_ext), before, after, outside
    )

    key_features = dot_nn(k_ref[...], map_ref[...]).astype(BF)
    tok = lax.broadcasted_iota(jnp.int32, (TILE, TILE), 0)
    carried = state[...]
    starts, features, inner = [], {}, {}
    for t in range(tiles):
        tl = slice(t * TILE, (t + 1) * TILE)
        starts.append(carried.astype(BF))
        carried = carried + dot_tn(key_features[tl, :], v_ref[tl, :])
    state[...] = carried

    def widen(t):
        sl = slice(t * rows, (t + 1) * rows)
        qs[sl, :] = q_ref[sl, :].astype(F32)

    def feature(t):
        features[t] = jnp.concatenate(
            [
                dot_nn(qs[pl.ds(t * rows + h, TILE, stride=heads), :].astype(BF), qmap_ref[h]).astype(BF)
                for h in range(heads)
            ],
            0,
        )

    def score(t):
        inner[t] = dot_nt(features[t], key_features[t * TILE : (t + 1) * TILE, :]).astype(BF) * keep[...]

    def combine(t):
        out = dot_nn(
            jnp.concatenate([inner.pop(t), features.pop(t)], 1),
            jnp.concatenate([v_ref[t * TILE : (t + 1) * TILE, :], starts[t]], 0),
        )
        factor = lax.rsqrt((tok + (first + t * TILE + 1)).astype(F32))
        for h in range(heads):
            os[pl.ds(t * rows + h, TILE, stride=heads), :] = out[h * TILE : (h + 1) * TILE, :] * factor

    def narrow(t):
        sl = slice(t * rows, (t + 1) * rows)
        o_ref[sl, :] = os[sl, :].astype(BF)

    apart = max(1, tiles // soft_tiles)

    def softmax_of(depth):
        def stage(t):
            if t % apart == 0 and t // apart < soft_tiles:
                soft[depth](t // apart)

        return stage

    def nothing(t):
        pass

    staged(
        tiles,
        lambda t: (softmax_of(0)(t), widen(t)),
        feature,
        lambda t: (softmax_of(1)(t), score(t)),
        combine,
        lambda t: (softmax_of(2)(t), narrow(t)),
    )


def per_device(ranks, queries, keys, values, query_maps, key_map, linear_cotangent):
    tokens, heads, head_dim = queries.shape
    chunk = CHUNK if tokens % CHUNK == 0 else W
    steps = tokens // chunk
    chunk_rows = chunk * heads
    tile_rows = TILE * heads
    slab = head_dim // ranks * heads
    params = pltpu.CompilerParams(vmem_limit_bytes=VMEM_LIMIT)
    q_rows = queries.reshape(tokens * heads, head_dim)
    c_rows = linear_cotangent.reshape(tokens * heads, head_dim)
    row_spec = pl.BlockSpec((chunk_rows, head_dim), lambda i: (i, 0))
    key_spec = pl.BlockSpec((chunk, head_dim), lambda i: (i, 0))

    def whole(shape):
        return pl.BlockSpec(shape, lambda i: (0,) * len(shape))

    packet = (ranks, head_dim + 2 * padded16(slab), head_dim)
    send, rim = pl.pallas_call(
        functools.partial(backward_kernel, heads, ranks, slab),
        grid=(steps,),
        in_specs=[row_spec, row_spec, key_spec, key_spec, whole(key_map.shape)],
        out_specs=[whole(packet), whole((2 * W, head_dim))],
        out_shape=[
            jax.ShapeDtypeStruct(packet, BF),
            jax.ShapeDtypeStruct((2 * W, head_dim), BF),
        ],
        scratch_shapes=[
            pltpu.VMEM((heads, head_dim, 2 * head_dim), F32),
            pltpu.VMEM((head_dim, head_dim), F32),
            pltpu.VMEM((tile_rows, TILE), BF),
            pltpu.VMEM((chunk_rows, head_dim), F32),
            pltpu.VMEM((chunk_rows, head_dim), F32),
            pltpu.VMEM((heads * head_dim, head_dim), F32),
            pltpu.VMEM((heads * head_dim, head_dim), F32),
        ],
        compiler_params=params,
        name="backward",
    )(q_rows, c_rows, keys, values, key_map)

    rim = lax.ppermute(rim, "seq", [(r, (r + 1) % ranks) for r in range(ranks)])
    got = lax.all_to_all(send, "seq", 0, 0)

    left_keys = pl.BlockSpec((W, head_dim), lambda i: (jnp.maximum(i * (chunk // W) - 1, 0), 0))
    bias = pltpu.VMEM((tile_rows, TILE), F32)
    soft_rows = pl.pallas_call(
        functools.partial(softmax_kernel, heads),
        grid=(steps,),
        in_specs=[row_spec, left_keys, key_spec, left_keys, key_spec],
        out_specs=row_spec,
        out_shape=jax.ShapeDtypeStruct(q_rows.shape, BF),
        scratch_shapes=[bias, bias],
        compiler_params=params,
        name="softmax",
    )(q_rows, keys, keys, values, values)

    soft_steps = max(n for n in (1, 2, 4) if n <= steps)
    soft_spec = pl.BlockSpec(
        (W // soft_steps * heads, head_dim), lambda i: (jnp.minimum(i, soft_steps - 1), 0)
    )
    in_vmem = pl.BlockSpec(memory_space=pltpu.VMEM)
    linear_rows, soft_rows, gradient = pl.pallas_call(
        functools.partial(forward_kernel, heads, ranks, slab, soft_steps),
        grid=(steps,),
        in_specs=[
            row_spec,
            key_spec,
            key_spec,
            whole(key_map.shape),
            whole(query_maps.shape),
            soft_spec,
            in_vmem,
            in_vmem,
            pl.BlockSpec(memory_space=pl.ANY),
        ],
        out_specs=[row_spec, soft_spec, whole((slab, head_dim))],
        out_shape=[
            jax.ShapeDtypeStruct(q_rows.shape, BF),
            jax.ShapeDtypeStruct(q_rows.shape, BF),
            jax.ShapeDtypeStruct((slab, head_dim), F32),
        ],
        scratch_shapes=[
            pltpu.VMEM((head_dim, head_dim), F32),
            pltpu.VMEM((tile_rows, TILE), BF),
            pltpu.VMEM((chunk_rows, head_dim), F32),
            pltpu.VMEM((chunk_rows, head_dim), F32),
            pltpu.VMEM((2 * W, head_dim), BF),
            pltpu.VMEM((2 * W, head_dim), BF),
            bias,
            bias,
        ],
        input_output_aliases={8: 1},
        compiler_params=params,
        name="forward",
    )(q_rows, keys, values, key_map, query_maps, q_rows, got, rim, soft_rows)

    return (
        soft_rows.reshape(queries.shape),
        linear_rows.reshape(queries.shape),
        gradient.reshape(head_dim // ranks, heads, head_dim),
    )


def solution(mesh):
    return jax.shard_map(
        functools.partial(per_device, mesh.shape["seq"]),
        mesh=mesh,
        in_specs=(
            P(("groups", "seq"), ("head", "rep"), None),
            P(("groups", "seq"), None),
            P(("groups", "seq"), None),
            P(("groups", "head", "rep"), None, None),
            P("groups", None),
            P(("groups", "seq"), ("head", "rep"), None),
        ),
        out_specs=(
            P(("groups", "seq"), ("head", "rep"), None),
            P(("groups", "seq"), ("head", "rep"), None),
            P(("groups", "seq"), ("head", "rep"), None),
        ),
        check_vma=False,
    )
```

time: 59.4 us -> 49.2 us (0.83)
  Pallas kernels: 46.5 us -> 40 us
  starting transfers between devices: 10.3 us -> 8.35 us
  local copies, waits for them, and re-layouts: 1.48 us -> 0 us
    pallas_call x2, Pallas kernels: 33.6 us -> 29.9 us  [the longest x1 16.7 us: per_device(): pl.pallas_call(functools.partial(softmax_kernel, heads), grid=(steps,), i...]
    pallas_call x1, Pallas kernels: 12.8 us -> 10.1 us  [per_device(): pl.pallas_call(functools.partial(backward_kernel, heads, ranks, slab), gr...]
    ppermute x1, starting transfers between devices: 3.93 us -> 2.02 us  [per_device(): rim = lax.ppermute(rim, 'seq', [(r, (r + 1) % ranks) for r in range(ranks)])]
    unnamed x4 -> x0, local copies, waits for them, and re-layouts: 1.48 us -> none
  transfers between devices with their start and end apart: 2 -> 2, of which waited for: 0 -> 0; matrix products, arithmetic and copies ran while one was open for 0% -> 0% of each run, Pallas kernels for 32% -> 34%
where the time goes in v2:
time: 49.2 us; the launch traced here: 49 us
  Pallas kernels  40 us (81%)
  starting transfers between devices  8.35 us (17%)
  between operations  0.64 us (1%)
    pallas_call x1, Pallas kernels, per_device(): pl.pallas_call(functools.partial(softmax_kernel, heads), grid=(steps,), i...  16.7 us
    pallas_call x1, Pallas kernels, per_device(): pl.pallas_call(functools.partial(forward_kernel, heads, ranks, slab, soft...  13.2 us
    pallas_call x1, Pallas kernels, per_device(): pl.pallas_call(functools.partial(backward_kernel, heads, ranks, slab), gr...  10.1 us
    all_to_all x1, starting transfers between devices, per_device(): got = lax.all_to_all(send, 'seq', 0, 0)  6.32 us
    ppermute x1, starting transfers between devices, per_device(): rim = lax.ppermute(rim, 'seq', [(r, (r + 1) % ranks) for r in range(ranks)])  2.02 us
  transfers between devices with their start and end apart: 2, of which 0 were waited for; matrix products, arithmetic and copies ran while one was open for 0% of the time, Pallas kernels for 34%

profile of v2, /device:TPU:0, one launch (start us, length us, event | category | flops | bytes accessed | tf_op | source)
XLA Modules:
  0.0 49.0 jit_solution(7461749520235248438)
XLA Ops:
  0.6 10.1 %backward.1 = (bf16[4,384,128]{2,1,0:T(8,128)(2,1)}, bf16[1024,128]{1,0:T(8,128)(2,1)}) custom-call(bf16[16384,128]{1,0:T(8,128)(2,1)} %bitcast.5, bf16[16384,128]{1,0:T(8,128)(2,1)} %bitcast.10, bf16[4096,128]{1,0:T(8,128)(2,1)} %k_ref.3, bf16[4096,128]{1,0:T(8,128)(2,1)} %v_ref.3, bf16[128,128]{1,0:T(8,128)(2,1)} %map_ref.3), custom_call_target="tpu_custom_call" | custom-call | tf_op jit(solution)/shard_map/backward/pallas_call | solution.py:333
  10.7 6.3 %all-to-all-start = ((bf16[4,384,128]{2,1,0:T(8,128)(2,1)}), bf16[4,384,128]{2,1,0:T(8,128)(2,1)}, u32[]{:S(2)}, u32[]{:S(2)}) async-start(bf16[4,384,128]{2,1,0:T(8,128)(2,1)} %get-tuple-element.8), calls=%async_computation | async-start | bytes 786432 | tf_op jit(solution)/shard_map/all_to_all | solution.py:356
  17.1 2.0 %collective-permute-start = (bf16[1024,128]{1,0:T(8,128)(2,1)}, bf16[1024,128]{1,0:T(8,128)(2,1)}, u32[]{:S(2)}, u32[]{:S(2)}) collective-permute-start(bf16[1024,128]{1,0:T(8,128)(2,1)} %get-tuple-element.9), channel_id=1, source_target_pairs={{0,4},{4,8},{8,12},{12,0},{1,5},{5,9},{9,13},{13,1},{2,6},{6,10},{... | collective-permute-start | bytes 786440 | tf_op jit(solution)/shard_map/ppermute | solution.py:355
  19.1 16.7 %softmax.1._ = bf16[16384,128]{1,0:T(8,128)(2,1)} custom-call(bf16[16384,128]{1,0:T(8,128)(2,1)} %bitcast.6, bf16[4096,128]{1,0:T(8,128)(2,1)} %k_ref.3, bf16[4096,128]{1,0:T(8,128)(2,1)} %k_ref.3, bf16[4096,128]{1,0:T(8,128)(2,1)} %v_ref.3, bf16[4096,128]{1,0:T(8,128)(2,1)} %v_ref.3), custom_call_target="tpu_custom_call" | custom-call | tf_op jit(solution)/shard_map/softmax/pallas_call | solution.py:360
  35.7 0.0 collective-permute-done.rim_ref
  35.7 0.0 all-to-all-done.got
  35.7 13.2 %forward.1 = (bf16[16384,128]{1,0:T(8,128)(2,1)}, bf16[16384,128]{1,0:T(8,128)(2,1)}, f32[128,128]{1,0:T(8,128)}) custom-call(bf16[16384,128]{1,0:T(8,128)(2,1)} %bitcast.7, bf16[4096,128]{1,0:T(8,128)(2,1)} %k_ref.3, bf16[4096,128]{1,0:T(8,128)(2,1)} %v_ref.3, bf16[128,128]{1,0:T(8,128)(2,1)} %map_ref.3, ...), custom_call_target="tpu_custom_call", output_to_operand_aliasing={{1}: (8, {})} | custom-call | tf_op jit(solution)/shard_map/forward/pallas_call | solution.py:376
Async XLA Ops:
  10.7 25.0 %all-to-all-start = ((bf16[4,384,128]{2,1,0:T(8,128)(2,1)}), bf16[4,384,128]{2,1,0:T(8,128)(2,1)}, u32[]{:S(2)}, u32[]{:S(2)}) async-start(bf16[4,384,128]{2,1,0:T(8,128)(2,1)} %get-tuple-element.8), calls=%async_computation | async-start | bytes 786432 | tf_op jit(solution)/shard_map/all_to_all | solution.py:356
  17.1 18.7 %collective-permute-start = (bf16[1024,128]{1,0:T(8,128)(2,1)}, bf16[1024,128]{1,0:T(8,128)(2,1)}, u32[]{:S(2)}, u32[]{:S(2)}) collective-permute-start(bf16[1024,128]{1,0:T(8,128)(2,1)} %get-tuple-element.9), channel_id=1, source_target_pairs={{0,4},{4,8},{8,12},{12,0},{1,5},{5,9},{9,13},{13,1},{2,6},{6,10},{... | collective-permute-start | bytes 786440 | tf_op jit(solution)/shard_map/ppermute | solution.py:355

commit v3 on v2

--- a/solution.py
+++ b/solution.py
@@ -10,7 +10,7 @@
 
 W = 512
 TILE = 128
-CHUNK = 1024
+CHUNKS = (1024, 1024, 1024)
 GROUP = 4
 BF = jnp.bfloat16
 F32 = jnp.float32
@@ -52,8 +52,9 @@
 
 
 def backward_kernel(
-    heads, ranks, slab, q_ref, c_ref, k_ref, v_ref, map_ref, send_ref, rim_ref, acc, state, keep, qs, cs, gi, qi
+    heads, ranks, slab, q_ref, c_ref, k_ref, v_ref, map_ref, *refs
 ):
+    send_refs, (acc, state, keep, qs, cs, gi, qi) = refs[:ranks], refs[ranks:]
     step, steps = pl.program_id(0), pl.num_programs(0)
     head_dim = map_ref.shape[0]
     tiles = k_ref.shape[0] // TILE
@@ -120,17 +121,18 @@
             pick = pl.ds(h, head_dim, stride=heads)
             gi[pick, :] = acc[h, :, :head_dim]
             qi[pick, :] = acc[h, :, head_dim:]
-        for d in range(ranks):
-            send_ref[d, :head_dim, :] = state[...].astype(BF)
+        size = padded16(slab)
+        for k, send_ref in enumerate(send_refs):
+            begin = pl.multiple_of(lax.rem(lax.axis_index("seq") + k, ranks) * slab, slab)
+            send_ref[:head_dim, :] = state[...].astype(BF)
             for n, terms in enumerate((gi, qi)):
-                part = terms[d * slab : (d + 1) * slab, :]
-                spare = padded16(slab) - slab
-                if spare:
-                    part = jnp.concatenate([part, jnp.zeros((spare, head_dim), F32)], 0)
-                begin = head_dim + n * padded16(slab)
-                send_ref[d, begin : begin + padded16(slab), :] = part.astype(BF)
-        rim_ref[:W, :] = k_ref[...][-W:, :]
-        rim_ref[W:, :] = v_ref[...][-W:, :]
+                part = terms[pl.ds(begin, slab), :]
+                if size > slab:
+                    part = jnp.concatenate([part, jnp.zeros((size - slab, head_dim), F32)], 0)
+                send_ref[head_dim + n * size : head_dim + (n + 1) * size, :] = part.astype(BF)
+        if ranks > 1:
+            send_refs[1][head_dim + 2 * size : head_dim + 2 * size + W, :] = k_ref[...][-W:, :]
+            send_refs[1][head_dim + 2 * size + W :, :] = v_ref[...][-W:, :]
 
 
 def window_biases(heads, before, after):
@@ -143,7 +145,7 @@
 def soft_stages(rows, q_ref, o_ref, keys_of, values_of, before, after, extra):
     head_dim = q_ref.shape[1]
     scale = float(LOG2E / np.sqrt(head_dim))
-    held = {}
+    held, total = {}, {}
 
     def score(t):
         held[t] = dot_nt(q_ref[t * rows : (t + 1) * rows, :], keys_of(t))
@@ -156,14 +158,13 @@
         if extra is not None:
             parts = [part if j == W // TILE else part + extra(t, j) for j, part in enumerate(parts)]
         highest = jnp.max(functools.reduce(jnp.maximum, parts), axis=1, keepdims=True)
-        held[t] = jnp.concatenate(
-            [jnp.exp2((part - highest) * scale).astype(BF) for part in parts], 1
-        )
+        weights = [jnp.exp2((part - highest) * scale) for part in parts]
+        total[t] = jnp.sum(functools.reduce(jnp.add, weights), axis=1, keepdims=True)
+        held[t] = jnp.concatenate([weight.astype(BF) for weight in weights], 1)
 
     def combine(t):
-        values = values_of(t)
-        both = dot_nn(held.pop(t), jnp.concatenate([values, jnp.ones_like(values)], 1))
-        o_ref[t * rows : (t + 1) * rows, :] = (both[:, :head_dim] / both[:, head_dim:]).astype(BF)
+        out = dot_nn(held.pop(t), values_of(t))
+        o_ref[t * rows : (t + 1) * rows, :] = (out / total.pop(t)).astype(BF)
 
     return score, weigh, combine
 
@@ -199,9 +200,10 @@
 
 
 def forward_kernel(
-    heads, ranks, slab, soft_steps, q_ref, k_ref, v_ref, map_ref, qmap_ref, soft_q_ref, got, rim_ref, _,
-    o_ref, soft_ref, grad_ref, state, keep, qs, os, keys_ext, values_ext, before, after
+    heads, ranks, slab, soft_steps, q_ref, k_ref, v_ref, map_ref, qmap_ref, soft_q_ref, *refs
 ):
+    got_refs, refs = refs[:ranks], refs[ranks + 1 :]
+    o_ref, soft_ref, grad_ref, state, keep, qs, os, got, keys_ext, values_ext, before, after = refs
     step, steps = pl.program_id(0), pl.num_programs(0)
     head_dim = map_ref.shape[0]
     tokens = k_ref.shape[0]
@@ -211,8 +213,12 @@
 
     @pl.when(step == 0)
     def _():
-        keys_ext[:W, :] = rim_ref[:W, :]
-        values_ext[:W, :] = rim_ref[W:, :]
+        size = padded16(slab)
+        length = head_dim + 2 * size
+        for k, got_ref in enumerate(got_refs):
+            got[lax.rem(rank - k + ranks, ranks)] = got_ref[:length, :]
+        keys_ext[:W, :] = got_refs[1][length : length + W, :]
+        values_ext[:W, :] = got_refs[1][length + W :, :]
         keys_ext[W:, :] = k_ref[:W, :]
         values_ext[W:, :] = v_ref[:W, :]
         window_biases(heads, before, after)
@@ -222,7 +228,7 @@
         grad = jnp.zeros((slab, head_dim), F32)
         for r in range(ranks):
             mine = jnp.where(rank == r, earlier, mine)
-            middle = head_dim + padded16(slab)
+            middle = head_dim + size
             grad = grad + got[r, head_dim:middle, :].astype(F32)[:slab]
             if r:
                 high = earlier.astype(BF)
@@ -267,13 +273,17 @@
         qs[sl, :] = q_ref[sl, :].astype(F32)
 
     def feature(t):
-        features[t] = jnp.concatenate(
-            [
-                dot_nn(qs[pl.ds(t * rows + h, TILE, stride=heads), :].astype(BF), qmap_ref[h]).astype(BF)
-                for h in range(heads)
-            ],
-            0,
-        )
+        if t % group:
+            return
+        count = min(group, tiles - t)
+        wide = [
+            dot_nn(
+                qs[pl.ds(t * rows + h, count * TILE, stride=heads), :].astype(BF), qmap_ref[h]
+            ).astype(BF)
+            for h in range(heads)
+        ]
+        for u in range(count):
+            features[t + u] = jnp.concatenate([x[u * TILE : (u + 1) * TILE, :] for x in wide], 0)
 
     def score(t):
         inner[t] = dot_nt(features[t], key_features[t * TILE : (t + 1) * TILE, :]).astype(BF) * keep[...]
@@ -292,6 +302,7 @@
         o_ref[sl, :] = os[sl, :].astype(BF)
 
     apart = max(1, tiles // soft_tiles)
+    group = min(GROUP, tiles)
 
     def softmax_of(depth):
         def stage(t):
@@ -306,6 +317,7 @@
     staged(
         tiles,
         lambda t: (softmax_of(0)(t), widen(t)),
+        *[lambda t: None] * (group - 1),
         feature,
         lambda t: (softmax_of(1)(t), score(t)),
         combine,
@@ -315,30 +327,29 @@
 
 def per_device(ranks, queries, keys, values, query_maps, key_map, linear_cotangent):
     tokens, heads, head_dim = queries.shape
-    chunk = CHUNK if tokens % CHUNK == 0 else W
-    steps = tokens // chunk
-    chunk_rows = chunk * heads
     tile_rows = TILE * heads
     slab = head_dim // ranks * heads
     params = pltpu.CompilerParams(vmem_limit_bytes=VMEM_LIMIT)
     q_rows = queries.reshape(tokens * heads, head_dim)
     c_rows = linear_cotangent.reshape(tokens * heads, head_dim)
-    row_spec = pl.BlockSpec((chunk_rows, head_dim), lambda i: (i, 0))
-    key_spec = pl.BlockSpec((chunk, head_dim), lambda i: (i, 0))
+
+    def split(chunk):
+        chunk = chunk if tokens % chunk == 0 else W
+        rows = pl.BlockSpec((chunk * heads, head_dim), lambda i: (i, 0))
+        return chunk, tokens // chunk, chunk * heads, rows, pl.BlockSpec((chunk, head_dim), lambda i: (i, 0))
 
     def whole(shape):
         return pl.BlockSpec(shape, lambda i: (0,) * len(shape))
 
-    packet = (ranks, head_dim + 2 * padded16(slab), head_dim)
-    send, rim = pl.pallas_call(
+    length = head_dim + 2 * padded16(slab)
+    packets = [(length + 2 * W if k == 1 else length, head_dim) for k in range(ranks)]
+    chunk, steps, chunk_rows, row_spec, key_spec = split(CHUNKS[0])
+    send = pl.pallas_call(
         functools.partial(backward_kernel, heads, ranks, slab),
         grid=(steps,),
         in_specs=[row_spec, row_spec, key_spec, key_spec, whole(key_map.shape)],
-        out_specs=[whole(packet), whole((2 * W, head_dim))],
-        out_shape=[
-            jax.ShapeDtypeStruct(packet, BF),
-            jax.ShapeDtypeStruct((2 * W, head_dim), BF),
-        ],
+        out_specs=[whole(packet) for packet in packets],
+        out_shape=[jax.ShapeDtypeStruct(packet, BF) for packet in packets],
         scratch_shapes=[
             pltpu.VMEM((heads, head_dim, 2 * head_dim), F32),
             pltpu.VMEM((head_dim, head_dim), F32),
@@ -352,10 +363,13 @@
         name="backward",
     )(q_rows, c_rows, keys, values, key_map)
 
-    rim = lax.ppermute(rim, "seq", [(r, (r + 1) % ranks) for r in range(ranks)])
-    got = lax.all_to_all(send, "seq", 0, 0)
-
-    left_keys = pl.BlockSpec((W, head_dim), lambda i: (jnp.maximum(i * (chunk // W) - 1, 0), 0))
+    got = [
+        lax.ppermute(part, "seq", [(r, (r + k) % ranks) for r in range(ranks)]) if k else part
+        for k, part in enumerate(send)
+    ]
+
+    chunk, steps, chunk_rows, row_spec, key_spec = split(CHUNKS[1])
+    left_keys = pl.BlockSpec((W, head_dim), lambda i, per=chunk // W: (jnp.maximum(i * per - 1, 0), 0))
     bias = pltpu.VMEM((tile_rows, TILE), F32)
     soft_rows = pl.pallas_call(
         functools.partial(softmax_kernel, heads),
@@ -368,6 +382,7 @@
         name="softmax",
     )(q_rows, keys, keys, values, values)
 
+    chunk, steps, chunk_rows, row_spec, key_spec = split(CHUNKS[2])
     soft_steps = max(n for n in (1, 2, 4) if n <= steps)
     soft_spec = pl.BlockSpec(
         (W // soft_steps * heads, head_dim), lambda i: (jnp.minimum(i, soft_steps - 1), 0)
@@ -383,8 +398,7 @@
             whole(key_map.shape),
             whole(query_maps.shape),
             soft_spec,
-            in_vmem,
-            in_vmem,
+            *[in_vmem] * ranks,
             pl.BlockSpec(memory_space=pl.ANY),
         ],
         out_specs=[row_spec, soft_spec, whole((slab, head_dim))],
@@ -398,15 +412,16 @@
             pltpu.VMEM((tile_rows, TILE), BF),
             pltpu.VMEM((chunk_rows, head_dim), F32),
             pltpu.VMEM((chunk_rows, head_dim), F32),
+            pltpu.VMEM((ranks, length, head_dim), BF),
             pltpu.VMEM((2 * W, head_dim), BF),
             pltpu.VMEM((2 * W, head_dim), BF),
             bias,
             bias,
         ],
-        input_output_aliases={8: 1},
+        input_output_aliases={6 + ranks: 1},
         compiler_params=params,
         name="forward",
-    )(q_rows, keys, values, key_map, query_maps, q_rows, got, rim, soft_rows)
+    )(q_rows, keys, values, key_map, query_maps, q_rows, *got, soft_rows)
 
     return (
         soft_rows.reshape(queries.shape),

time: 49.2 us -> 46.8 us (0.951)
  starting transfers between devices: 8.35 us -> 6.96 us
  Pallas kernels: 40 us -> 39.1 us
    all_to_all x1 -> x0, starting transfers between devices: 6.32 us -> none  [per_device(): got = lax.all_to_all(send, 'seq', 0, 0)]
    ppermute x1 -> x3, starting transfers between devices: 2.02 us -> 6.96 us  [per_device(): lax.ppermute(part, 'seq', [(r, (r + k) % ranks) for r in range(ranks)])]
    pallas_call x1, Pallas kernels: 16.7 us -> 15.8 us  [per_device(): pl.pallas_call(functools.partial(softmax_kernel, heads), grid=(steps,), i...]
  transfers between devices with their start and end apart: 2 -> 3, of which waited for: 0 -> 0; matrix products, arithmetic and copies ran while one was open for 0% -> 0% of each run, Pallas kernels for 34% -> 34%
where the time goes in v3:
time: 46.8 us; the launch traced here: 46.7 us
  Pallas kernels  39.1 us (84%)
  starting transfers between devices  6.96 us (15%)
  between operations  0.64 us (1%)
    pallas_call x1, Pallas kernels, per_device(): pl.pallas_call(functools.partial(softmax_kernel, heads), grid=(steps,), i...  15.8 us
    pallas_call x1, Pallas kernels, per_device(): pl.pallas_call(functools.partial(forward_kernel, heads, ranks, slab, soft...  13.2 us
    pallas_call x1, Pallas kernels, per_device(): pl.pallas_call(functools.partial(backward_kernel, heads, ranks, slab), gr...  10.1 us
    ppermute x3, starting transfers between devices, per_device(): lax.ppermute(part, 'seq', [(r, (r + k) % ranks) for r in range(ranks)])  6.96 us
  transfers between devices with their start and end apart: 3, of which 0 were waited for; matrix products, arithmetic and copies ran while one was open for 0% of the time, Pallas kernels for 34%

profile of v3, /device:TPU:0, one launch (start us, length us, event | category | flops | bytes accessed | tf_op | source)
XLA Modules:
  0.0 46.7 jit_solution(2187625914859972610)
XLA Ops:
  0.6 10.1 %backward.1 = (bf16[384,128]{1,0:T(8,128)(2,1)}, bf16[1408,128]{1,0:T(8,128)(2,1)}, bf16[384,128]{1,0:T(8,128)(2,1)}, bf16[384,128]{1,0:T(8,128)(2,1)}) custom-call(bf16[16384,128]{1,0:T(8,128)(2,1)} %bitcast.5, bf16[16384,128]{1,0:T(8,128)(2,1)} %bitcast.10, bf16[4096,128]{1,0:T(8,128)(2,1)} %k_ref.3, bf16[4096,128]{1,0:T(8,128)(2,1)} %v_ref.3, ...), custom_call_target="tpu_custom_call" | custom-call | tf_op jit(solution)/shard_map/backward/pallas_call | solution.py:347
  10.7 3.0 %collective-permute-start = (bf16[1408,128]{1,0:T(8,128)(2,1)}, bf16[1408,128]{1,0:T(8,128)(2,1)}, u32[]{:S(2)}, u32[]{:S(2)}) collective-permute-start(bf16[1408,128]{1,0:T(8,128)(2,1)} %get-tuple-element.11), channel_id=1, source_target_pairs={{0,4},{4,8},{8,12},{12,0},{1,5},{5,9},{9,13},{13,1},{2,6},{6,10},{... | collective-permute-start | bytes 1081352 | tf_op jit(solution)/shard_map/ppermute | solution.py:367
  13.7 2.6 %collective-permute-start.1 = (bf16[384,128]{1,0:T(8,128)(2,1)}, bf16[384,128]{1,0:T(8,128)(2,1)}, u32[]{:S(2)}, u32[]{:S(2)}) collective-permute-start(bf16[384,128]{1,0:T(8,128)(2,1)} %get-tuple-element.12), channel_id=1, source_target_pairs={{0,8},{4,12},{8,0},{12,4},{1,9},{5,13},{9,1},{13,5},{2,10},{6,14},... | collective-permute-start | bytes 294920 | tf_op jit(solution)/shard_map/ppermute | solution.py:367
  16.3 1.3 %collective-permute-start.2 = (bf16[384,128]{1,0:T(8,128)(2,1)}, bf16[384,128]{1,0:T(8,128)(2,1)}, u32[]{:S(2)}, u32[]{:S(2)}) collective-permute-start(bf16[384,128]{1,0:T(8,128)(2,1)} %get-tuple-element.13), channel_id=1, source_target_pairs={{0,12},{4,0},{8,4},{12,8},{1,13},{5,1},{9,5},{13,9},{2,14},{6,2},{... | collective-permute-start | bytes 294920 | tf_op jit(solution)/shard_map/ppermute | solution.py:367
  17.7 15.8 %softmax.1.refs_4_ = bf16[16384,128]{1,0:T(8,128)(2,1)} custom-call(bf16[16384,128]{1,0:T(8,128)(2,1)} %bitcast.6, bf16[4096,128]{1,0:T(8,128)(2,1)} %k_ref.3, bf16[4096,128]{1,0:T(8,128)(2,1)} %k_ref.3, bf16[4096,128]{1,0:T(8,128)(2,1)} %v_ref.3, bf16[4096,128]{1,0:T(8,128)(2,1)} %v_ref.3), custom_call_target="tpu_custom_call" | custom-call | tf_op jit(solution)/shard_map/softmax/pallas_call | solution.py:374
  33.5 0.0 collective-permute-done.1.refs_2_
  33.5 0.0 collective-permute-done.2.refs_3_
  33.5 0.0 collective-permute-done.refs_1_
  33.5 13.2 %forward.1 = (bf16[16384,128]{1,0:T(8,128)(2,1)}, bf16[16384,128]{1,0:T(8,128)(2,1)}, f32[128,128]{1,0:T(8,128)}) custom-call(bf16[16384,128]{1,0:T(8,128)(2,1)} %bitcast.7, bf16[4096,128]{1,0:T(8,128)(2,1)} %k_ref.3, bf16[4096,128]{1,0:T(8,128)(2,1)} %v_ref.3, bf16[128,128]{1,0:T(8,128)(2,1)} %map_ref.3, ...), custom_call_target="tpu_custom_call", output_to_operand_aliasing={{1}: (10, {})} | custom-call | tf_op jit(solution)/shard_map/forward/pallas_call | solution.py:391
Async XLA Ops:
  10.7 22.8 %collective-permute-start = (bf16[1408,128]{1,0:T(8,128)(2,1)}, bf16[1408,128]{1,0:T(8,128)(2,1)}, u32[]{:S(2)}, u32[]{:S(2)}) collective-permute-start(bf16[1408,128]{1,0:T(8,128)(2,1)} %get-tuple-element.11), channel_id=1, source_target_pairs={{0,4},{4,8},{8,12},{12,0},{1,5},{5,9},{9,13},{13,1},{2,6},{6,10},{... | collective-permute-start | bytes 1081352 | tf_op jit(solution)/shard_map/ppermute | solution.py:367
  13.7 19.8 %collective-permute-start.1 = (bf16[384,128]{1,0:T(8,128)(2,1)}, bf16[384,128]{1,0:T(8,128)(2,1)}, u32[]{:S(2)}, u32[]{:S(2)}) collective-permute-start(bf16[384,128]{1,0:T(8,128)(2,1)} %get-tuple-element.12), channel_id=1, source_target_pairs={{0,8},{4,12},{8,0},{12,4},{1,9},{5,13},{9,1},{13,5},{2,10},{6,14},... | collective-permute-start | bytes 294920 | tf_op jit(solution)/shard_map/ppermute | solution.py:367
  16.3 17.2 %collective-permute-start.2 = (bf16[384,128]{1,0:T(8,128)(2,1)}, bf16[384,128]{1,0:T(8,128)(2,1)}, u32[]{:S(2)}, u32[]{:S(2)}) collective-permute-start(bf16[384,128]{1,0:T(8,128)(2,1)} %get-tuple-element.13), channel_id=1, source_target_pairs={{0,12},{4,0},{8,4},{12,8},{1,13},{5,1},{9,5},{13,9},{2,14},{6,2},{... | collective-permute-start | bytes 294920 | tf_op jit(solution)/shard_map/ppermute | solution.py:367

commit v4 on v3

--- a/solution.py
+++ b/solution.py
@@ -59,7 +59,7 @@
     head_dim = map_ref.shape[0]
     tiles = k_ref.shape[0] // TILE
     rows = TILE * heads
-    group = min(GROUP, tiles)
+    group = tiles
 
     @pl.when(step == 0)
     def _():
@@ -135,15 +135,17 @@
             send_refs[1][head_dim + 2 * size + W :, :] = v_ref[...][-W:, :]
 
 
-def window_biases(heads, before, after):
+def window_masks(heads, late, keep_first, keep_last):
     rows = TILE * heads
-    low = lax.broadcasted_iota(jnp.int32, (rows, TILE), 1) <= tokens_of_rows(rows, heads)
-    before[...] = jnp.where(low, -1e30, 0.0)
-    after[...] = jnp.where(low, 0.0, -1e30)
-
-
-def soft_stages(rows, q_ref, o_ref, keys_of, values_of, before, after, extra):
+    causal = lax.broadcasted_iota(jnp.int32, (rows, TILE), 1) <= tokens_of_rows(rows, heads)
+    late[...] = jnp.where(causal, 1.0, 0.0)
+    keep_last[...] = late[...].astype(BF)
+    keep_first[...] = (1.0 - late[...]).astype(BF)
+
+
+def soft_stages(rows, q_ref, o_ref, keys_of, values_of, masks, extra):
     head_dim = q_ref.shape[1]
+    late, keep_first, keep_last = masks
     scale = float(LOG2E / np.sqrt(head_dim))
     held, total = {}, {}
 
@@ -153,14 +155,14 @@
     def weigh(t):
         scores = held[t]
         parts = [scores[:, j * TILE : (j + 1) * TILE] for j in range(W // TILE + 1)]
-        parts[0] = parts[0] + before[...]
-        parts[-1] = parts[-1] + after[...]
         if extra is not None:
             parts = [part if j == W // TILE else part + extra(t, j) for j, part in enumerate(parts)]
+        parts = [jnp.where(late[...] > 0.5, parts[-1], parts[0]), *parts[1:-1]]
         highest = jnp.max(functools.reduce(jnp.maximum, parts), axis=1, keepdims=True)
         weights = [jnp.exp2((part - highest) * scale) for part in parts]
         total[t] = jnp.sum(functools.reduce(jnp.add, weights), axis=1, keepdims=True)
-        held[t] = jnp.concatenate([weight.astype(BF) for weight in weights], 1)
+        ends, *middle = [weight.astype(BF) for weight in weights]
+        held[t] = jnp.concatenate([ends * keep_first[...], *middle, ends * keep_last[...]], 1)
 
     def combine(t):
         out = dot_nn(held.pop(t), values_of(t))
@@ -169,41 +171,25 @@
     return score, weigh, combine
 
 
-def softmax_kernel(heads, q_ref, kb_ref, kh_ref, vb_ref, vh_ref, o_ref, before, after):
+def softmax_kernel(heads, q_ref, k_ref, v_ref, o_ref, *masks):
     @pl.when(pl.program_id(0) == 0)
     def _():
-        window_biases(heads, before, after)
-
-    def window(left, here):
-        def of(t):
-            start, end = t * TILE, (t + 1) * TILE
-            if start >= W:
-                return here[start - W : end, :]
-            return jnp.concatenate([left[start:, :], here[:end, :]], 0)
-
-        return of
+        window_masks(heads, *masks)
+
+    def window(ref):
+        return lambda t: ref[t * TILE : (t + 1) * TILE + W, :]
 
     stages = soft_stages(
-        TILE * heads, q_ref, o_ref, window(kb_ref, kh_ref), window(vb_ref, vh_ref), before, after, None
-    )
-    count = kh_ref.shape[0] // TILE
-    skipped = W // TILE
-
-    @pl.when(pl.program_id(0) == 0)
-    def _():
-        if count > skipped:
-            staged(count - skipped, *(lambda t, stage=stage: stage(t + skipped) for stage in stages))
-
-    @pl.when(pl.program_id(0) > 0)
-    def _():
-        staged(count, *stages)
+        TILE * heads, q_ref, o_ref, window(k_ref), window(v_ref), masks, None
+    )
+    staged((k_ref.shape[0] - W) // TILE, *stages)
 
 
 def forward_kernel(
     heads, ranks, slab, soft_steps, q_ref, k_ref, v_ref, map_ref, qmap_ref, soft_q_ref, *refs
 ):
     got_refs, refs = refs[:ranks], refs[ranks + 1 :]
-    o_ref, soft_ref, grad_ref, state, keep, qs, os, got, keys_ext, values_ext, before, after = refs
+    o_ref, soft_ref, grad_ref, state, keep, qs, os, got, keys_ext, values_ext, *masks = refs
     step, steps = pl.program_id(0), pl.num_programs(0)
     head_dim = map_ref.shape[0]
     tokens = k_ref.shape[0]
@@ -221,7 +207,7 @@
         values_ext[:W, :] = got_refs[1][length + W :, :]
         keys_ext[W:, :] = k_ref[:W, :]
         values_ext[W:, :] = v_ref[:W, :]
-        window_biases(heads, before, after)
+        window_masks(heads, *masks)
         keep[...] = causal_keep(heads)
         earlier = jnp.zeros((head_dim, head_dim), F32)
         mine = earlier
@@ -255,7 +241,7 @@
         return jnp.where(jnp.logical_and(rank == 0, early), -1e30, 0.0)
 
     soft = soft_stages(
-        rows, soft_q_ref, soft_ref, window(keys_ext), window(values_ext), before, after, outside
+        rows, soft_q_ref, soft_ref, window(keys_ext), window(values_ext), masks, outside
     )
 
     key_features = dot_nn(k_ref[...], map_ref[...]).astype(BF)
@@ -368,19 +354,26 @@
         for k, part in enumerate(send)
     ]
 
-    chunk, steps, chunk_rows, row_spec, key_spec = split(CHUNKS[1])
-    left_keys = pl.BlockSpec((W, head_dim), lambda i, per=chunk // W: (jnp.maximum(i * per - 1, 0), 0))
-    bias = pltpu.VMEM((tile_rows, TILE), F32)
+    tiles = (tokens - W) // TILE
+    per_step = max(n for n in range(1, CHUNKS[1] // TILE + 1) if tiles % n == 0)
+    chunk = per_step * TILE
+    later_rows = pl.BlockSpec(
+        (pl.Element(chunk * heads), pl.Element(head_dim)), lambda i: (pl.multiple_of((W + i * chunk) * heads, TILE), 0)
+    )
+    window_keys = pl.BlockSpec(
+        (pl.Element(W + chunk), pl.Element(head_dim)), lambda i: (pl.multiple_of(i * chunk, TILE), 0)
+    )
+    masks = [pltpu.VMEM((tile_rows, TILE), kind) for kind in (F32, BF, BF)]
     soft_rows = pl.pallas_call(
         functools.partial(softmax_kernel, heads),
-        grid=(steps,),
-        in_specs=[row_spec, left_keys, key_spec, left_keys, key_spec],
-        out_specs=row_spec,
+        grid=(tiles // per_step,),
+        in_specs=[later_rows, window_keys, window_keys],
+        out_specs=later_rows,
         out_shape=jax.ShapeDtypeStruct(q_rows.shape, BF),
-        scratch_shapes=[bias, bias],
+        scratch_shapes=masks,
         compiler_params=params,
         name="softmax",
-    )(q_rows, keys, keys, values, values)
+    )(q_rows, keys, values)
 
     chunk, steps, chunk_rows, row_spec, key_spec = split(CHUNKS[2])
     soft_steps = max(n for n in (1, 2, 4) if n <= steps)
@@ -398,7 +391,7 @@
             whole(key_map.shape),
             whole(query_maps.shape),
             soft_spec,
-            *[in_vmem] * ranks,
+            *[whole(packet) for packet in packets],
             pl.BlockSpec(memory_space=pl.ANY),
         ],
         out_specs=[row_spec, soft_spec, whole((slab, head_dim))],
@@ -415,8 +408,7 @@
             pltpu.VMEM((ranks, length, head_dim), BF),
             pltpu.VMEM((2 * W, head_dim), BF),
             pltpu.VMEM((2 * W, head_dim), BF),
-            bias,
-            bias,
+            *masks,
         ],
         input_output_aliases={6 + ranks: 1},
         compiler_params=params,

time: 46.8 us -> 45.1 us (0.964)
  Pallas kernels: 39.1 us -> 37.3 us
    pallas_call x1, Pallas kernels: 15.8 us -> 14.6 us  [per_device(): pl.pallas_call(functools.partial(softmax_kernel, heads), grid=(tiles // p...]
  transfers between devices with their start and end apart: 3 -> 3, of which waited for: 0 -> 0; matrix products, arithmetic and copies ran while one was open for 0% -> 0% of each run, Pallas kernels for 34% -> 33%
where the time goes in v4:
time: 45.1 us; the launch traced here: 45 us
  Pallas kernels  37.3 us (83%)
  starting transfers between devices  7 us (16%)
  between operations  0.64 us (1%)
    pallas_call x1, Pallas kernels, per_device(): pl.pallas_call(functools.partial(softmax_kernel, heads), grid=(tiles // p...  14.6 us
    pallas_call x1, Pallas kernels, per_device(): pl.pallas_call(functools.partial(forward_kernel, heads, ranks, slab, soft...  12.9 us
    pallas_call x1, Pallas kernels, per_device(): pl.pallas_call(functools.partial(backward_kernel, heads, ranks, slab), gr...  9.85 us
    ppermute x3, starting transfers between devices, per_device(): lax.ppermute(part, 'seq', [(r, (r + k) % ranks) for r in range(ranks)])  7 us
  transfers between devices with their start and end apart: 3, of which 0 were waited for; matrix products, arithmetic and copies ran while one was open for 0% of the time, Pallas kernels for 33%

profile of v4, /device:TPU:0, one launch (start us, length us, event | category | flops | bytes accessed | tf_op | source)
XLA Modules:
  0.0 45.0 jit_solution(12661192502758552956)
XLA Ops:
  0.6 9.8 %backward.1 = (bf16[384,128]{1,0:T(8,128)(2,1)}, bf16[1408,128]{1,0:T(8,128)(2,1)}, bf16[384,128]{1,0:T(8,128)(2,1)}, bf16[384,128]{1,0:T(8,128)(2,1)}) custom-call(bf16[16384,128]{1,0:T(8,128)(2,1)} %bitcast.5, bf16[16384,128]{1,0:T(8,128)(2,1)} %bitcast.10, bf16[4096,128]{1,0:T(8,128)(2,1)} %k_ref.5, bf16[4096,128]{1,0:T(8,128)(2,1)} %v_ref.5, ...), custom_call_target="tpu_custom_call" | custom-call | tf_op jit(solution)/shard_map/backward/pallas_call | solution.py:333
  10.5 3.0 %collective-permute-start = (bf16[1408,128]{1,0:T(8,128)(2,1)}, bf16[1408,128]{1,0:T(8,128)(2,1)}, u32[]{:S(2)}, u32[]{:S(2)}) collective-permute-start(bf16[1408,128]{1,0:T(8,128)(2,1)} %get-tuple-element.11), channel_id=1, source_target_pairs={{0,4},{4,8},{8,12},{12,0},{1,5},{5,9},{9,13},{13,1},{2,6},{6,10},{... | collective-permute-start | bytes 1081352 | tf_op jit(solution)/shard_map/ppermute | solution.py:353
  13.5 2.6 %collective-permute-start.1 = (bf16[384,128]{1,0:T(8,128)(2,1)}, bf16[384,128]{1,0:T(8,128)(2,1)}, u32[]{:S(2)}, u32[]{:S(2)}) collective-permute-start(bf16[384,128]{1,0:T(8,128)(2,1)} %get-tuple-element.12), channel_id=1, source_target_pairs={{0,8},{4,12},{8,0},{12,4},{1,9},{5,13},{9,1},{13,5},{2,10},{6,14},... | collective-permute-start | bytes 294920 | tf_op jit(solution)/shard_map/ppermute | solution.py:353
  16.1 1.4 %collective-permute-start.2 = (bf16[384,128]{1,0:T(8,128)(2,1)}, bf16[384,128]{1,0:T(8,128)(2,1)}, u32[]{:S(2)}, u32[]{:S(2)}) collective-permute-start(bf16[384,128]{1,0:T(8,128)(2,1)} %get-tuple-element.13), channel_id=1, source_target_pairs={{0,12},{4,0},{8,4},{12,8},{1,13},{5,1},{9,5},{13,9},{2,14},{6,2},{... | collective-permute-start | bytes 294920 | tf_op jit(solution)/shard_map/ppermute | solution.py:353
  17.5 14.6 %softmax.1.refs_4_ = bf16[16384,128]{1,0:T(8,128)(2,1)} custom-call(bf16[16384,128]{1,0:T(8,128)(2,1)} %bitcast.6, bf16[4096,128]{1,0:T(8,128)(2,1)} %k_ref.5, bf16[4096,128]{1,0:T(8,128)(2,1)} %v_ref.5), custom_call_target="tpu_custom_call" | custom-call | tf_op jit(solution)/shard_map/softmax/pallas_call | solution.py:367
  32.1 0.0 collective-permute-done.1.refs_2_
  32.1 0.0 collective-permute-done.2.refs_3_
  32.1 0.0 collective-permute-done.refs_1_
  32.1 12.9 %forward.1 = (bf16[16384,128]{1,0:T(8,128)(2,1)}, bf16[16384,128]{1,0:T(8,128)(2,1)}, f32[128,128]{1,0:T(8,128)}) custom-call(bf16[16384,128]{1,0:T(8,128)(2,1)} %bitcast.7, bf16[4096,128]{1,0:T(8,128)(2,1)} %k_ref.5, bf16[4096,128]{1,0:T(8,128)(2,1)} %v_ref.5, bf16[128,128]{1,0:T(8,128)(2,1)} %map_ref.3, ...), custom_call_target="tpu_custom_call", output_to_operand_aliasing={{1}: (10, {})} | custom-call | tf_op jit(solution)/shard_map/forward/pallas_call | solution.py:384
Async XLA Ops:
  10.5 21.6 %collective-permute-start = (bf16[1408,128]{1,0:T(8,128)(2,1)}, bf16[1408,128]{1,0:T(8,128)(2,1)}, u32[]{:S(2)}, u32[]{:S(2)}) collective-permute-start(bf16[1408,128]{1,0:T(8,128)(2,1)} %get-tuple-element.11), channel_id=1, source_target_pairs={{0,4},{4,8},{8,12},{12,0},{1,5},{5,9},{9,13},{13,1},{2,6},{6,10},{... | collective-permute-start | bytes 1081352 | tf_op jit(solution)/shard_map/ppermute | solution.py:353
  13.5 18.6 %collective-permute-start.1 = (bf16[384,128]{1,0:T(8,128)(2,1)}, bf16[384,128]{1,0:T(8,128)(2,1)}, u32[]{:S(2)}, u32[]{:S(2)}) collective-permute-start(bf16[384,128]{1,0:T(8,128)(2,1)} %get-tuple-element.12), channel_id=1, source_target_pairs={{0,8},{4,12},{8,0},{12,4},{1,9},{5,13},{9,1},{13,5},{2,10},{6,14},... | collective-permute-start | bytes 294920 | tf_op jit(solution)/shard_map/ppermute | solution.py:353
  16.1 16.0 %collective-permute-start.2 = (bf16[384,128]{1,0:T(8,128)(2,1)}, bf16[384,128]{1,0:T(8,128)(2,1)}, u32[]{:S(2)}, u32[]{:S(2)}) collective-permute-start(bf16[384,128]{1,0:T(8,128)(2,1)} %get-tuple-element.13), channel_id=1, source_target_pairs={{0,12},{4,0},{8,4},{12,8},{1,13},{5,1},{9,5},{13,9},{2,14},{6,2},{... | collective-permute-start | bytes 294920 | tf_op jit(solution)/shard_map/ppermute | solution.py:353

commit v5 on v4

--- a/solution.py
+++ b/solution.py
@@ -10,8 +10,9 @@
 
 W = 512
 TILE = 128
-CHUNKS = (1024, 1024, 1024)
+CHUNKS = (1024, 1024)
 GROUP = 4
+CUTS = (0, 2, 6, 12, 20)
 BF = jnp.bfloat16
 F32 = jnp.float32
 LOG2E = 1.4426950408889634
@@ -36,6 +37,12 @@
 
 def padded16(rows):
     return -(-rows // 16) * 16
+
+
+def breadth(count, *stages):
+    for stage in stages:
+        for t in range(count):
+            stage(t)
 
 
 def staged(count, *stages):
@@ -113,7 +120,7 @@
             )
             acc[h] += dot_tn((part(qs, begin, h, group * TILE) * factor).astype(BF), right)
 
-    staged(tiles, widen, score, gradient, gather)
+    breadth(tiles, widen, score, gradient, gather)
 
     @pl.when(step == steps - 1)
     def _():
@@ -157,7 +164,7 @@
         parts = [scores[:, j * TILE : (j + 1) * TILE] for j in range(W // TILE + 1)]
         if extra is not None:
             parts = [part if j == W // TILE else part + extra(t, j) for j, part in enumerate(parts)]
-        parts = [jnp.where(late[...] > 0.5, parts[-1], parts[0]), *parts[1:-1]]
+        parts = [jnp.where(lax.broadcasted_iota(jnp.int32, (rows, TILE), 1) <= lax.broadcasted_iota(jnp.int32, (rows, TILE), 0) // (rows // TILE), parts[-1], parts[0]), *parts[1:-1]]
         highest = jnp.max(functools.reduce(jnp.maximum, parts), axis=1, keepdims=True)
         weights = [jnp.exp2((part - highest) * scale) for part in parts]
         total[t] = jnp.sum(functools.reduce(jnp.add, weights), axis=1, keepdims=True)
@@ -171,18 +178,58 @@
     return score, weigh, combine
 
 
-def softmax_kernel(heads, q_ref, k_ref, v_ref, o_ref, *masks):
-    @pl.when(pl.program_id(0) == 0)
-    def _():
-        window_masks(heads, *masks)
+def softmax_kernel(
+    heads, cuts, q_hbm, k_hbm, v_hbm, o_hbm, late, keep_first, keep_last, q_all, k_all, v_all, o_all, ins, outs
+):
+    rows = TILE * heads
+    tiles = q_all.shape[0] // rows
+
+    def piece(n):
+        begin, end = cuts[n], cuts[n + 1] if n + 1 < len(cuts) else tiles
+        left = begin * TILE + W if n else 0
+        right = end * TILE + W
+        return [
+            pltpu.make_async_copy(
+                q_hbm.at[W * heads + begin * rows : W * heads + end * rows],
+                q_all.at[begin * rows : end * rows],
+                ins.at[0, n],
+            ),
+            pltpu.make_async_copy(k_hbm.at[left:right], k_all.at[left:right], ins.at[1, n]),
+            pltpu.make_async_copy(v_hbm.at[left:right], v_all.at[left:right], ins.at[2, n]),
+        ]
+
+    def result(t):
+        return pltpu.make_async_copy(
+            o_all.at[t * rows : (t + 1) * rows],
+            o_hbm.at[W * heads + t * rows : W * heads + (t + 1) * rows],
+            outs.at[t],
+        )
+
+    for n in range(len(cuts)):
+        for copy in piece(n):
+            copy.start()
+    window_masks(heads, late, keep_first, keep_last)
 
     def window(ref):
         return lambda t: ref[t * TILE : (t + 1) * TILE + W, :]
 
-    stages = soft_stages(
-        TILE * heads, q_ref, o_ref, window(k_ref), window(v_ref), masks, None
-    )
-    staged((k_ref.shape[0] - W) // TILE, *stages)
+    score, weigh, combine = soft_stages(
+        rows, q_all, o_all, window(k_all), window(v_all), (late, keep_first, keep_last), None
+    )
+
+    def first(t):
+        if t in cuts:
+            for copy in piece(cuts.index(t)):
+                copy.wait()
+        score(t)
+
+    def last(t):
+        combine(t)
+        result(t).start()
+
+    staged(tiles, first, weigh, last)
+    for t in range(tiles):
+        result(t).wait()
 
 
 def forward_kernel(
@@ -300,7 +347,7 @@
     def nothing(t):
         pass
 
-    staged(
+    breadth(
         tiles,
         lambda t: (softmax_of(0)(t), widen(t)),
         *[lambda t: None] * (group - 1),
@@ -355,27 +402,28 @@
     ]
 
     tiles = (tokens - W) // TILE
-    per_step = max(n for n in range(1, CHUNKS[1] // TILE + 1) if tiles % n == 0)
-    chunk = per_step * TILE
-    later_rows = pl.BlockSpec(
-        (pl.Element(chunk * heads), pl.Element(head_dim)), lambda i: (pl.multiple_of((W + i * chunk) * heads, TILE), 0)
-    )
-    window_keys = pl.BlockSpec(
-        (pl.Element(W + chunk), pl.Element(head_dim)), lambda i: (pl.multiple_of(i * chunk, TILE), 0)
-    )
+    cuts = [t for t in CUTS if t < tiles]
     masks = [pltpu.VMEM((tile_rows, TILE), kind) for kind in (F32, BF, BF)]
+    in_hbm = pl.BlockSpec(memory_space=pl.ANY)
     soft_rows = pl.pallas_call(
-        functools.partial(softmax_kernel, heads),
-        grid=(tiles // per_step,),
-        in_specs=[later_rows, window_keys, window_keys],
-        out_specs=later_rows,
+        functools.partial(softmax_kernel, heads, cuts),
+        in_specs=[in_hbm] * 3,
+        out_specs=in_hbm,
         out_shape=jax.ShapeDtypeStruct(q_rows.shape, BF),
-        scratch_shapes=masks,
+        scratch_shapes=[
+            *masks,
+            pltpu.VMEM((tiles * tile_rows, head_dim), BF),
+            pltpu.VMEM(keys.shape, BF),
+            pltpu.VMEM(keys.shape, BF),
+            pltpu.VMEM((tiles * tile_rows, head_dim), BF),
+            pltpu.SemaphoreType.DMA((3, len(cuts))),
+            pltpu.SemaphoreType.DMA((tiles,)),
+        ],
         compiler_params=params,
         name="softmax",
     )(q_rows, keys, values)
 
-    chunk, steps, chunk_rows, row_spec, key_spec = split(CHUNKS[2])
+    chunk, steps, chunk_rows, row_spec, key_spec = split(CHUNKS[1])
     soft_steps = max(n for n in (1, 2, 4) if n <= steps)
     soft_spec = pl.BlockSpec(
         (W // soft_steps * heads, head_dim), lambda i: (jnp.minimum(i, soft_steps - 1), 0)

time: 45.1 us -> 44.3 us (0.982)
  Pallas kernels: 37.3 us -> 36.4 us
    pallas_call x1, Pallas kernels: 12.9 us -> 12.3 us  [per_device(): pl.pallas_call(functools.partial(forward_kernel, heads, ranks, slab, soft...]
  transfers between devices with their start and end apart: 3 -> 3, of which waited for: 0 -> 0; matrix products, arithmetic and copies ran while one was open for 0% -> 0% of each run, Pallas kernels for 33% -> 32%
where the time goes in v5:
time: 44.3 us; the launch traced here: 44.1 us
  Pallas kernels  36.4 us (82%)
  starting transfers between devices  6.96 us (16%)
  between operations  0.8 us (2%)
    pallas_call x1, Pallas kernels, per_device(): pl.pallas_call(functools.partial(softmax_kernel, heads, cuts), in_specs=[...  14.2 us
    pallas_call x1, Pallas kernels, per_device(): pl.pallas_call(functools.partial(forward_kernel, heads, ranks, slab, soft...  12.3 us
    pallas_call x1, Pallas kernels, per_device(): pl.pallas_call(functools.partial(backward_kernel, heads, ranks, slab), gr...  9.87 us
    ppermute x3, starting transfers between devices, per_device(): lax.ppermute(part, 'seq', [(r, (r + k) % ranks) for r in range(ranks)])  6.96 us
  transfers between devices with their start and end apart: 3, of which 0 were waited for; matrix products, arithmetic and copies ran while one was open for 0% of the time, Pallas kernels for 32%

profile of v5, /device:TPU:0, one launch (start us, length us, event | category | flops | bytes accessed | tf_op | source)
XLA Modules:
  0.0 44.1 jit_solution(3886861509966746935)
XLA Ops:
  0.6 9.9 %backward.1 = (bf16[384,128]{1,0:T(8,128)(2,1)}, bf16[1408,128]{1,0:T(8,128)(2,1)}, bf16[384,128]{1,0:T(8,128)(2,1)}, bf16[384,128]{1,0:T(8,128)(2,1)}) custom-call(bf16[16384,128]{1,0:T(8,128)(2,1)} %bitcast.5, bf16[16384,128]{1,0:T(8,128)(2,1)} %bitcast.10, bf16[4096,128]{1,0:T(8,128)(2,1)} %k_ref.3, bf16[4096,128]{1,0:T(8,128)(2,1)} %v_ref.3, ...), custom_call_target="tpu_custom_call" | custom-call | tf_op jit(solution)/shard_map/backward/pallas_call | solution.py:380
  10.5 3.0 %collective-permute-start = (bf16[1408,128]{1,0:T(8,128)(2,1)}, bf16[1408,128]{1,0:T(8,128)(2,1)}, u32[]{:S(2)}, u32[]{:S(2)}) collective-permute-start(bf16[1408,128]{1,0:T(8,128)(2,1)} %get-tuple-element.11), channel_id=1, source_target_pairs={{0,4},{4,8},{8,12},{12,0},{1,5},{5,9},{9,13},{13,1},{2,6},{6,10},{... | collective-permute-start | bytes 1081352 | tf_op jit(solution)/shard_map/ppermute | solution.py:400
  13.5 2.6 %collective-permute-start.1 = (bf16[384,128]{1,0:T(8,128)(2,1)}, bf16[384,128]{1,0:T(8,128)(2,1)}, u32[]{:S(2)}, u32[]{:S(2)}) collective-permute-start(bf16[384,128]{1,0:T(8,128)(2,1)} %get-tuple-element.12), channel_id=1, source_target_pairs={{0,8},{4,12},{8,0},{12,4},{1,9},{5,13},{9,1},{13,5},{2,10},{6,14},... | collective-permute-start | bytes 294920 | tf_op jit(solution)/shard_map/ppermute | solution.py:400
  16.1 1.3 %collective-permute-start.2 = (bf16[384,128]{1,0:T(8,128)(2,1)}, bf16[384,128]{1,0:T(8,128)(2,1)}, u32[]{:S(2)}, u32[]{:S(2)}) collective-permute-start(bf16[384,128]{1,0:T(8,128)(2,1)} %get-tuple-element.13), channel_id=1, source_target_pairs={{0,12},{4,0},{8,4},{12,8},{1,13},{5,1},{9,5},{13,9},{2,14},{6,2},{... | collective-permute-start | bytes 294920 | tf_op jit(solution)/shard_map/ppermute | solution.py:400
  17.5 14.2 %softmax.1.refs_4_ = bf16[16384,128]{1,0:T(8,128)(2,1)} custom-call(bf16[16384,128]{1,0:T(8,128)(2,1)} %bitcast.6, bf16[4096,128]{1,0:T(8,128)(2,1)} %k_ref.3, bf16[4096,128]{1,0:T(8,128)(2,1)} %v_ref.3), custom_call_target="tpu_custom_call" | custom-call | tf_op jit(solution)/shard_map/softmax/pallas_call | solution.py:408
  31.7 0.0 collective-permute-done.1.refs_2_
  31.7 0.0 collective-permute-done.2.refs_3_
  31.7 0.0 collective-permute-done.refs_1_
  31.7 12.3 %forward.1 = (bf16[16384,128]{1,0:T(8,128)(2,1)}, bf16[16384,128]{1,0:T(8,128)(2,1)}, f32[128,128]{1,0:T(8,128)}) custom-call(bf16[16384,128]{1,0:T(8,128)(2,1)} %bitcast.7, bf16[4096,128]{1,0:T(8,128)(2,1)} %k_ref.3, bf16[4096,128]{1,0:T(8,128)(2,1)} %v_ref.3, bf16[128,128]{1,0:T(8,128)(2,1)} %map_ref.3, ...), custom_call_target="tpu_custom_call", output_to_operand_aliasing={{1}: (10, {})} | custom-call | tf_op jit(solution)/shard_map/forward/pallas_call | solution.py:432
Async XLA Ops:
  10.5 21.2 %collective-permute-start = (bf16[1408,128]{1,0:T(8,128)(2,1)}, bf16[1408,128]{1,0:T(8,128)(2,1)}, u32[]{:S(2)}, u32[]{:S(2)}) collective-permute-start(bf16[1408,128]{1,0:T(8,128)(2,1)} %get-tuple-element.11), channel_id=1, source_target_pairs={{0,4},{4,8},{8,12},{12,0},{1,5},{5,9},{9,13},{13,1},{2,6},{6,10},{... | collective-permute-start | bytes 1081352 | tf_op jit(solution)/shard_map/ppermute | solution.py:400
  13.5 18.2 %collective-permute-start.1 = (bf16[384,128]{1,0:T(8,128)(2,1)}, bf16[384,128]{1,0:T(8,128)(2,1)}, u32[]{:S(2)}, u32[]{:S(2)}) collective-permute-start(bf16[384,128]{1,0:T(8,128)(2,1)} %get-tuple-element.12), channel_id=1, source_target_pairs={{0,8},{4,12},{8,0},{12,4},{1,9},{5,13},{9,1},{13,5},{2,10},{6,14},... | collective-permute-start | bytes 294920 | tf_op jit(solution)/shard_map/ppermute | solution.py:400
  16.1 15.6 %collective-permute-start.2 = (bf16[384,128]{1,0:T(8,128)(2,1)}, bf16[384,128]{1,0:T(8,128)(2,1)}, u32[]{:S(2)}, u32[]{:S(2)}) collective-permute-start(bf16[384,128]{1,0:T(8,128)(2,1)} %get-tuple-element.13), channel_id=1, source_target_pairs={{0,12},{4,0},{8,4},{12,8},{1,13},{5,1},{9,5},{13,9},{2,14},{6,2},{... | collective-permute-start | bytes 294920 | tf_op jit(solution)/shard_map/ppermute | solution.py:400

commit v6 on v5

--- a/solution.py
+++ b/solution.py
@@ -205,7 +205,7 @@
             outs.at[t],
         )
 
-    for n in range(len(cuts)):
+    for n in range(min(2, len(cuts))):
         for copy in piece(n):
             copy.start()
     window_masks(heads, late, keep_first, keep_last)
@@ -219,8 +219,12 @@
 
     def first(t):
         if t in cuts:
-            for copy in piece(cuts.index(t)):
+            n = cuts.index(t)
+            for copy in piece(n):
                 copy.wait()
+            if n + 2 < len(cuts):
+                for copy in piece(n + 2):
+                    copy.start()
         score(t)
 
     def last(t):

time: 44.3 us -> 44.3 us (level)
  no operation moved by 1% of the time
where the time goes in v6:
time: 44.3 us; the launch traced here: 44.1 us
  Pallas kernels  36.4 us (82%)
  starting transfers between devices  6.96 us (16%)
  between operations  0.8 us (2%)
    pallas_call x1, Pallas kernels, per_device(): pl.pallas_call(functools.partial(softmax_kernel, heads, cuts), in_specs=[...  14.2 us
    pallas_call x1, Pallas kernels, per_device(): pl.pallas_call(functools.partial(forward_kernel, heads, ranks, slab, soft...  12.3 us
    pallas_call x1, Pallas kernels, per_device(): pl.pallas_call(functools.partial(backward_kernel, heads, ranks, slab), gr...  9.87 us
    ppermute x3, starting transfers between devices, per_device(): lax.ppermute(part, 'seq', [(r, (r + k) % ranks) for r in range(ranks)])  6.96 us
  transfers between devices with their start and end apart: 3, of which 0 were waited for; matrix products, arithmetic and copies ran while one was open for 0% of the time, Pallas kernels for 32%

profile of v6, /device:TPU:0, one launch (start us, length us, event | category | flops | bytes accessed | tf_op | source)
XLA Modules:
  0.0 44.1 jit_solution(1740780054292340372)
XLA Ops:
  0.6 9.9 %backward.1 = (bf16[384,128]{1,0:T(8,128)(2,1)}, bf16[1408,128]{1,0:T(8,128)(2,1)}, bf16[384,128]{1,0:T(8,128)(2,1)}, bf16[384,128]{1,0:T(8,128)(2,1)}) custom-call(bf16[16384,128]{1,0:T(8,128)(2,1)} %bitcast.5, bf16[16384,128]{1,0:T(8,128)(2,1)} %bitcast.10, bf16[4096,128]{1,0:T(8,128)(2,1)} %k_ref.3, bf16[4096,128]{1,0:T(8,128)(2,1)} %v_ref.3, ...), custom_call_target="tpu_custom_call" | custom-call | tf_op jit(solution)/shard_map/backward/pallas_call | solution.py:384
  10.5 3.0 %collective-permute-start = (bf16[1408,128]{1,0:T(8,128)(2,1)}, bf16[1408,128]{1,0:T(8,128)(2,1)}, u32[]{:S(2)}, u32[]{:S(2)}) collective-permute-start(bf16[1408,128]{1,0:T(8,128)(2,1)} %get-tuple-element.11), channel_id=1, source_target_pairs={{0,4},{4,8},{8,12},{12,0},{1,5},{5,9},{9,13},{13,1},{2,6},{6,10},{... | collective-permute-start | bytes 1081352 | tf_op jit(solution)/shard_map/ppermute | solution.py:404
  13.5 2.6 %collective-permute-start.1 = (bf16[384,128]{1,0:T(8,128)(2,1)}, bf16[384,128]{1,0:T(8,128)(2,1)}, u32[]{:S(2)}, u32[]{:S(2)}) collective-permute-start(bf16[384,128]{1,0:T(8,128)(2,1)} %get-tuple-element.12), channel_id=1, source_target_pairs={{0,8},{4,12},{8,0},{12,4},{1,9},{5,13},{9,1},{13,5},{2,10},{6,14},... | collective-permute-start | bytes 294920 | tf_op jit(solution)/shard_map/ppermute | solution.py:404
  16.1 1.3 %collective-permute-start.2 = (bf16[384,128]{1,0:T(8,128)(2,1)}, bf16[384,128]{1,0:T(8,128)(2,1)}, u32[]{:S(2)}, u32[]{:S(2)}) collective-permute-start(bf16[384,128]{1,0:T(8,128)(2,1)} %get-tuple-element.13), channel_id=1, source_target_pairs={{0,12},{4,0},{8,4},{12,8},{1,13},{5,1},{9,5},{13,9},{2,14},{6,2},{... | collective-permute-start | bytes 294920 | tf_op jit(solution)/shard_map/ppermute | solution.py:404
  17.5 14.2 %softmax.1.refs_4_ = bf16[16384,128]{1,0:T(8,128)(2,1)} custom-call(bf16[16384,128]{1,0:T(8,128)(2,1)} %bitcast.6, bf16[4096,128]{1,0:T(8,128)(2,1)} %k_ref.3, bf16[4096,128]{1,0:T(8,128)(2,1)} %v_ref.3), custom_call_target="tpu_custom_call" | custom-call | tf_op jit(solution)/shard_map/softmax/pallas_call | solution.py:412
  31.7 0.0 collective-permute-done.1.refs_2_
  31.7 0.0 collective-permute-done.2.refs_3_
  31.7 0.0 collective-permute-done.refs_1_
  31.7 12.3 %forward.1 = (bf16[16384,128]{1,0:T(8,128)(2,1)}, bf16[16384,128]{1,0:T(8,128)(2,1)}, f32[128,128]{1,0:T(8,128)}) custom-call(bf16[16384,128]{1,0:T(8,128)(2,1)} %bitcast.7, bf16[4096,128]{1,0:T(8,128)(2,1)} %k_ref.3, bf16[4096,128]{1,0:T(8,128)(2,1)} %v_ref.3, bf16[128,128]{1,0:T(8,128)(2,1)} %map_ref.3, ...), custom_call_target="tpu_custom_call", output_to_operand_aliasing={{1}: (10, {})} | custom-call | tf_op jit(solution)/shard_map/forward/pallas_call | solution.py:436
Async XLA Ops:
  10.5 21.2 %collective-permute-start = (bf16[1408,128]{1,0:T(8,128)(2,1)}, bf16[1408,128]{1,0:T(8,128)(2,1)}, u32[]{:S(2)}, u32[]{:S(2)}) collective-permute-start(bf16[1408,128]{1,0:T(8,128)(2,1)} %get-tuple-element.11), channel_id=1, source_target_pairs={{0,4},{4,8},{8,12},{12,0},{1,5},{5,9},{9,13},{13,1},{2,6},{6,10},{... | collective-permute-start | bytes 1081352 | tf_op jit(solution)/shard_map/ppermute | solution.py:404
  13.5 18.2 %collective-permute-start.1 = (bf16[384,128]{1,0:T(8,128)(2,1)}, bf16[384,128]{1,0:T(8,128)(2,1)}, u32[]{:S(2)}, u32[]{:S(2)}) collective-permute-start(bf16[384,128]{1,0:T(8,128)(2,1)} %get-tuple-element.12), channel_id=1, source_target_pairs={{0,8},{4,12},{8,0},{12,4},{1,9},{5,13},{9,1},{13,5},{2,10},{6,14},... | collective-permute-start | bytes 294920 | tf_op jit(solution)/shard_map/ppermute | solution.py:404
  16.1 15.6 %collective-permute-start.2 = (bf16[384,128]{1,0:T(8,128)(2,1)}, bf16[384,128]{1,0:T(8,128)(2,1)}, u32[]{:S(2)}, u32[]{:S(2)}) collective-permute-start(bf16[384,128]{1,0:T(8,128)(2,1)} %get-tuple-element.13), channel_id=1, source_target_pairs={{0,12},{4,0},{8,4},{12,8},{1,13},{5,1},{9,5},{13,9},{2,14},{6,2},{... | collective-permute-start | bytes 294920 | tf_op jit(solution)/shard_map/ppermute | solution.py:404
